TPU v7x, 128 devices: a whole 4x4x4 slice. The times are simulated.
128 devices in a mesh: cam: 32 (over y, x, core), lidar: 4 (over z).
Axes of the slice: x: 4, y: 4, z: 4, core: 2. Of those that a mesh axis runs over, the one named last changes fastest.
Arguments:
- key_feats: bfloat16 [8192, 128, 256], P(('cam', 'lidar')), may hold values from -6 to 6
- query_feats: bfloat16 [512, 128, 256], P(('cam', 'lidar')), may hold values from -6 to 6
- key_dest: int32 [8192], P(('cam', 'lidar')), may hold values from 0 to 127, as said below
- key_scene: int32 [8192], P(('cam', 'lidar')), may hold values from 0 to 3
- key_count: int32 [8192], P(('cam', 'lidar')), may hold values from 16 to 128, as said below
- pos_tile: int32 [512], P(('cam', 'lidar')), may hold values from 0 to 8191, as said below
- pos_row: int32 [512, 128], P(('cam', 'lidar')), may hold values from 0 to 127, as said below
Outputs:
- query_loss: float32 [512, 128], P(('cam', 'lidar'))
- key_grad: bfloat16 [8192, 128, 256], P(('cam', 'lidar'))
Inputs may be any that keep to these rules, and one draw needn't show every extreme that they name: `key_dest`: the 64 key tiles of one device go to 64 different devices; each device gets a tile from the device with index one lower (cyclically), and one device gets a tile from every device. `key_count`: the first key tile of each device is full. pos_tile[i] is a key tile with key_dest equal to the owner of query tile i; a query tile takes its scene from that key tile, so tiles of one device may share a scene. pos_row[i, r] < key_count[pos_tile[i]].
All inputs are finite; a program needn't handle non-finite values.
Results may differ from a plain program's by a relative error of at most 0.0053.
Values may be sent and summed in bfloat16 or wider, within the bound.
No kernel may reach another device: no remote copies, remote signals or barrier semaphores. Data moves between devices by JAX's collectives and lax.ppermute only.
A program may use at most 192 MiB of HBM per device.

v0:
```python
import math

import jax
import jax.numpy as jnp
from jax import lax
from jax.sharding import PartitionSpec as P

inv_temp = 1.0 / 0.07
eps = 1e-06


def unit_rows(x):
    xf = x.astype(jnp.float32)
    scaled = (
        xf * lax.rsqrt(jnp.mean(xf * xf, axis=-1, keepdims=True) + eps) / math.sqrt(x.shape[-1])
    )
    return scaled.astype(jnp.bfloat16)


def shards(key_feats, query_feats, key_dest, key_scene, key_count, pos_tile, pos_row):
    tiles, rows, width = key_feats.shape
    query_tiles = query_feats.shape[0]
    n_cam = lax.axis_size("cam")
    n_lidar = lax.axis_size("lidar")
    devices = n_cam * n_lidar
    myself = lax.axis_index("cam") * n_lidar + lax.axis_index("lidar")
    device_iota = jnp.arange(devices, dtype=jnp.int32)
    owner = key_dest[None, :] == device_iota[:, None]
    owner_bf = owner.astype(jnp.bfloat16)
    normed = unit_rows(key_feats).reshape(tiles, rows * width)
    packed = jnp.dot(owner_bf, normed, preferred_element_type=jnp.float32).astype(jnp.bfloat16)
    packed = packed.reshape(devices, rows, width)
    tile_ids = myself * tiles + jnp.arange(tiles, dtype=jnp.int32)
    labels = jnp.stack([tile_ids + 1, key_scene, key_count], axis=1)
    routed_labels = jnp.sum(jnp.where(owner[:, :, None], labels[None, :, :], 0), axis=1)
    arrived, tags = (
        lax.all_to_all(packed, ("cam", "lidar"), split_axis=0, concat_axis=0, tiled=True),
        lax.all_to_all(routed_labels, ("cam", "lidar"), split_axis=0, concat_axis=0, tiled=True),
    )
    slot_tile = tags[:, 0] - 1
    slot_scene = tags[:, 1]
    slot_count = tags[:, 2]
    row_iota = jnp.arange(rows, dtype=jnp.int32)
    key_ok = (row_iota[None, :] < slot_count[:, None]).reshape(-1)
    key_block = arrived.reshape(devices * rows, width)
    key_scene_rows = jnp.repeat(slot_scene, rows)
    hit = slot_tile[None, :] == pos_tile[:, None]
    q_scene = jnp.sum(jnp.where(hit, slot_scene[None, :], 0), axis=1)
    q_slot = jnp.sum(jnp.where(hit, device_iota[None, :], 0), axis=1)
    q_column = (q_slot[:, None] * rows + pos_row).reshape(-1)
    q_scene_rows = jnp.repeat(q_scene, rows)
    normq = unit_rows(query_feats).reshape(query_tiles * rows, width)
    per_block = min(query_tiles, max(1, 512 // rows))
    blocks = query_tiles // per_block
    column_iota = jnp.arange(devices * rows, dtype=jnp.int32)

    def one_block(grad, part):
        queries, scenes, column = part
        logits = (
            jnp.einsum("qe,ke->qk", queries, key_block, preferred_element_type=jnp.float32)
            * inv_temp
        )
        allowed = key_ok[None, :] & (key_scene_rows[None, :] == scenes[:, None])
        expo = jnp.where(allowed, jnp.exp(logits), 0.0)
        total = jnp.sum(expo, axis=1)
        picked = jnp.take_along_axis(logits, column[:, None], axis=1)[:, 0]
        loss = jnp.log(total) - picked
        target = (column_iota[None, :] == column[:, None]).astype(jnp.float32)
        weights = (expo / total[:, None] - target).astype(jnp.bfloat16)
        grad = grad + jnp.einsum("qk,qe->ke", weights, queries, preferred_element_type=jnp.float32)
        return (grad, loss)

    grad, losses = lax.scan(
        one_block,
        jnp.zeros((devices * rows, width), jnp.float32),
        (
            normq.reshape(blocks, per_block * rows, width),
            q_scene_rows.reshape(blocks, per_block * rows),
            q_column.reshape(blocks, per_block * rows),
        ),
    )
    outgoing = (grad * inv_temp).astype(jnp.bfloat16).reshape(devices, rows, width)
    returned = lax.all_to_all(outgoing, ("cam", "lidar"), split_axis=0, concat_axis=0, tiled=True)
    returned = returned.reshape(devices, rows * width)
    key_grad = jnp.dot(owner_bf.T, returned, preferred_element_type=jnp.float32).astype(
        jnp.bfloat16
    )
    return (losses.reshape(query_tiles, rows), key_grad.reshape(tiles, rows, width))


def solution(mesh):
    return jax.shard_map(
        shards,
        mesh=mesh,
        in_specs=(
            P(("cam", "lidar"), None, None),
            P(("cam", "lidar"), None, None),
            P(("cam", "lidar")),
            P(("cam", "lidar")),
            P(("cam", "lidar")),
            P(("cam", "lidar")),
            P(("cam", "lidar"), None),
        ),
        out_specs=(P(("cam", "lidar"), None), P(("cam", "lidar"), None, None)),
        check_vma=False,
    )
```

profile of v0, /device:TPU:1, one launch (start us, length us, event | category | flops | bytes accessed | tf_op | source)
XLA Modules:
  0.0 325.8 jit_solution(13002096098963023121)
XLA Ops:
  0.6 0.7 iota_compare_fusion.2
  1.4 0.7 pad_add_fusion
  2.2 0.8 copy.13
  2.9 11.5 %all-to-all-start = ((s32[128,1,3]{2,1,0:T(1,128)}), s32[128,1,3]{2,1,0:T(1,128)S(1)}, u32[]{:S(2)}, u32[]{:S(2)}) async-start(s32[128,1,3]{2,1,0:T(1,128)} %copy.13), calls=%async_computation | async-start | bytes 131072 | tf_op jit(solution)/shard_map/all_to_all | solution.py:38
  14.4 3.3 %fusion.3 = f32[64,128]{1,0:T(8,128)S(1)} fusion(bf16[64,128,256]{2,1,0:T(8,128)(2,1)} %param.7), kind=kLoop, calls=%fused_computation.13 | loop fusion | flops 6283264 | bytes 4227072 | tf_op jit(solution)/shard_map/reduce_sum | solution.py:15
  17.8 2.9 fusion.5
  20.7 2.6 copy.14
  23.3 5.7 %convolution_convert_fusion = bf16[128,32768]{1,0:T(8,128)(2,1)} fusion(bf16[64,32768]{1,0:T(8,128)(2,1)S(1)} %bitcast.43, s32[64]{0:T(128)S(1)} %copy-done.2), kind=kOutput, calls=%fused_computation.1 | convolution fusion | flops 541073408 | bytes 12583168 | tf_op jit(solution)/shard_map/dot_general | solution.py:31
  29.0 9.1 %copy.15 = bf16[16,8,128,256]{3,2,1,0:T(8,128)(2,1)} copy(bf16[16,8,128,256]{3,1,2,0:T(8,128)(2,1)} %bitcast.40) | data formatting | bytes 16777216
  38.1 10.2 %all-to-all-start.1 = ((bf16[128,128,256]{2,1,0:T(8,128)(2,1)}), bf16[128,128,256]{2,1,0:T(8,128)(2,1)}, u32[]{:S(2)}, u32[]{:S(2)}) async-start(bf16[128,128,256]{2,1,0:T(8,128)(2,1)} %bitcast.39), calls=%async_computation.1 | async-start | bytes 16777216 | tf_op jit(solution)/shard_map/all_to_all | solution.py:37
  48.3 0.1 fusion.6
  48.5 0.1 fusion.8
  48.6 0.2 slice_reduce_fusion.1
  48.9 0.2 fusion.13
  49.4 101.6 %all-to-all-done.1 = bf16[128,128,256]{2,1,0:T(8,128)(2,1)} async-done(((bf16[128,128,256]{2,1,0:T(8,128)(2,1)}), bf16[128,128,256]{2,1,0:T(8,128)(2,1)}, u32[]{:S(2)}, u32[]{:S(2)}) %all-to-all-start.1) | async-done | bytes 8388640 | tf_op jit(solution)/shard_map/all_to_all | solution.py:37
  150.9 20.1 %fusion = (f32[512]{0:T(512)S(1)}, f32[512,16384]{1,0:T(8,128)}) fusion(s32[16384]{0:T(1024)S(1)} %broadcast_bitcast_fusion, s32[512]{0:T(512)S(1)} %broadcast_bitcast_fusion.1, pred[16384]{0:T(1024)(128)(4,1)S(1)} %fusion.10, bf16[512,256]{1,0:T(8,128)(2,1)S(1)} %bitcast.48, bf16[16384,256]{1,0:T(8,128)(2,1)} %bitcast.8), kind=kOutput, calls=%fused_computation.7 | convolution fusion | flops 4336909824 | bytes 42291200 | tf_op jit(solution)/shard_map/while/body/eval_jaxpr/qe,ke->qk/dot_general | solution.py:60
  171.1 23.2 %fusion.1 = bf16[16384,256]{1,0:T(8,128)(2,1)} fusion(bf16[512,256]{1,0:T(8,128)(2,1)S(1)} %bitcast.49, f32[512,16384]{1,0:T(8,128)} %get-tuple-element.28, s32[512]{0:T(512)S(1)} %fusion.25, f32[512]{0:T(512)S(1)} %get-tuple-element.27, s32[16384]{0:T(1024)S(1)} %broadcast_bitcast_fusion, s32[512]{0:T(512)S(1)} %broadcast_bitcast_fusion.1, ...), kind=kOutput, calls=%fused_computation.9 | convolution fusion | flops 4370464768 | bytes 42293248 | tf_op jit(solution)/shard_map/while/body/eval_jaxpr/qk,qe->ke/dot_general | solution.py:70
  194.3 8.8 %all-to-all-start.2 = ((bf16[128,128,256]{2,1,0:T(8,128)(2,1)}), bf16[128,128,256]{2,1,0:T(8,128)(2,1)}, u32[]{:S(2)}, u32[]{:S(2)}) async-start(bf16[128,128,256]{2,1,0:T(8,128)(2,1)} %bitcast.45), calls=%async_computation.2 | async-start | bytes 16777216 | tf_op jit(solution)/shard_map/all_to_all | solution.py:83
  203.2 8.5 %gather_fusion = f32[512]{0:T(512)S(1)} fusion(f32[512,16384]{1,0:T(8,128)} %get-tuple-element.28, s32[512]{0:T(512)S(1)} %bitcast.38), kind=kCustom, calls=%fused_computation | custom fusion | bytes 8192 | tf_op jit(solution)/shard_map/while/body/eval_jaxpr/jit(take_along_axis)/gather | solution.py:66
  211.7 0.7 fusion.18
  212.3 93.4 %all-to-all-done.2 = bf16[128,128,256]{2,1,0:T(8,128)(2,1)} async-done(((bf16[128,128,256]{2,1,0:T(8,128)(2,1)}), bf16[128,128,256]{2,1,0:T(8,128)(2,1)}, u32[]{:S(2)}, u32[]{:S(2)}) %all-to-all-start.2) | async-done | bytes 8388640 | tf_op jit(solution)/shard_map/all_to_all | solution.py:83
  305.7 12.3 %copy.16 = bf16[16,8,128,256]{3,1,2,0:T(8,128)(2,1)} copy(bf16[16,8,128,256]{3,2,1,0:T(8,128)(2,1)} %bitcast.20) | data formatting | bytes 16777216
  318.0 4.7 %convolution_convert_fusion.1 = bf16[64,32768]{1,0:T(8,128)(2,1)S(1)} fusion(bf16[128,32768]{1,0:T(8,128)(2,1)} %bitcast.41, s32[64]{0:T(128)S(1)} %copy-done.2), kind=kOutput, calls=%fused_computation.2 | convolution fusion | flops 538976256 | bytes 12583168 | tf_op jit(solution)/shard_map/dot_general | solution.py:85
  322.7 3.1 copy.17
  (23 shorter events, 0.6 us)
Async XLA Ops:
  2.9 35.1 %all-to-all-start = ((s32[128,1,3]{2,1,0:T(1,128)}), s32[128,1,3]{2,1,0:T(1,128)S(1)}, u32[]{:S(2)}, u32[]{:S(2)}) async-start(s32[128,1,3]{2,1,0:T(1,128)} %copy.13), calls=%async_computation | async-start | bytes 131072 | tf_op jit(solution)/shard_map/all_to_all | solution.py:38
  17.8 5.5 %copy-start.2 = (s32[64]{0:T(128)S(1)}, s32[64]{0:T(128)}, u32[]{:S(2)}) copy-start(s32[64]{0:T(128)} %param.9) | copy-start | bytes 772
  38.1 10.3 %copy-start = (bf16[4,128,256]{2,1,0:T(8,128)(2,1)S(1)}, bf16[4,128,256]{2,1,0:T(8,128)(2,1)}, u32[]{:S(2)}) copy-start(bf16[4,128,256]{2,1,0:T(8,128)(2,1)} %param.8) | copy-start | bytes 786436
  38.1 10.8 %copy-start.3 = (s32[4]{0:T(128)S(1)}, s32[4]{0:T(128)}, u32[]{:S(2)}) copy-start(s32[4]{0:T(128)} %param.12) | copy-start | bytes 52
  38.1 11.1 %copy-start.1 = (s32[4,128]{1,0:T(4,128)S(1)}, s32[4,128]{1,0:T(4,128)}, u32[]{:S(2)}) copy-start(s32[4,128]{1,0:T(4,128)} %param.13) | copy-start | bytes 6148
  38.1 112.9 %all-to-all-start.1 = ((bf16[128,128,256]{2,1,0:T(8,128)(2,1)}), bf16[128,128,256]{2,1,0:T(8,128)(2,1)}, u32[]{:S(2)}, u32[]{:S(2)}) async-start(bf16[128,128,256]{2,1,0:T(8,128)(2,1)} %bitcast.39), calls=%async_computation.1 | async-start | bytes 16777216 | tf_op jit(solution)/shard_map/all_to_all | solution.py:37
  194.3 111.4 %all-to-all-start.2 = ((bf16[128,128,256]{2,1,0:T(8,128)(2,1)}), bf16[128,128,256]{2,1,0:T(8,128)(2,1)}, u32[]{:S(2)}, u32[]{:S(2)}) async-start(bf16[128,128,256]{2,1,0:T(8,128)(2,1)} %bitcast.45), calls=%async_computation.2 | async-start | bytes 16777216 | tf_op jit(solution)/shard_map/all_to_all | solution.py:83
where the time goes:
time: 327 us; the launch traced here: 326 us
  waiting for transfers between devices  195 us (60%)
  matrix products  53.7 us (16%)
  local copies, waits for them, and re-layouts  36.5 us (11%)
  starting transfers between devices  30.5 us (9%)
  other arithmetic  9.36 us (3%)
    all_to_all x1, waiting for transfers between devices, shards(): lax.all_to_all(packed, ('cam', 'lidar'), split_axis=0, concat_axis=0, til...  102 us
    all_to_all x1, waiting for transfers between devices, shards(): lax.all_to_all(outgoing, ('cam', 'lidar'), split_axis=0, concat_axis=0, t...  93.4 us
    unnamed x13, local copies, waits for them, and re-layouts  27.2 us
    dot_general x1, matrix products, one_block(): jnp.einsum('qk,qe->ke', weights, queries, preferred_element_type=jnp.floa...  23.2 us
    dot_general x1, matrix products, one_block(): jnp.einsum('qe,ke->qk', queries, key_block, preferred_element_type=jnp.fl...  20.1 us
    all_to_all x1, starting transfers between devices, shards(): lax.all_to_all(routed_labels, ('cam', 'lidar'), split_axis=0, concat_axis...  11.5 us
    all_to_all x1, starting transfers between devices, shards(): lax.all_to_all(packed, ('cam', 'lidar'), split_axis=0, concat_axis=0, til...  10.2 us
    all_to_all x1, starting transfers between devices, shards(): lax.all_to_all(outgoing, ('cam', 'lidar'), split_axis=0, concat_axis=0, t...  8.76 us
  transfers between devices with their start and end apart: 3, of which 2 were waited for; matrix products, arithmetic and copies ran while one was open for 10% of the time, Pallas kernels for 0%

commit v1 on v0

v1 whole, which is shorter than its diff:
```python
import math

import jax
import jax.numpy as jnp
from jax import lax
from jax.experimental import pallas as pl
from jax.experimental.pallas import tpu as pltpu
from jax.sharding import PartitionSpec as P

inv_temp = 1.0 / 0.07
log2_scale = inv_temp * math.log2(math.e)
eps = 1e-06
GROUP = 4
AXES = ("cam", "lidar")


def unit_rows(x):
    xf = x.astype(jnp.float32)
    scaled = (
        xf * lax.rsqrt(jnp.mean(xf * xf, axis=-1, keepdims=True) + eps) / math.sqrt(x.shape[-1])
    )
    return scaled.astype(jnp.bfloat16)


def exchange(x):
    return lax.all_to_all(x, AXES, split_axis=0, concat_axis=0, tiled=True)


def products(keys, queries):
    return lax.dot_general(
        keys, queries, (((1,), (1,)), ((), ())), preferred_element_type=jnp.float32
    )


def total_kernel(dest, count, nk_ref, *rest):
    q_refs, code_ref, out_ref = rest[:GROUP], rest[GROUP], rest[GROUP + 1]
    rows = nk_ref.shape[1]
    lanes = code_ref.shape[2]
    step = pl.program_id(0)

    @pl.when(step == 0)
    def _():
        out_ref[...] = jnp.zeros_like(out_ref)

    row = lax.broadcasted_iota(jnp.int32, (rows, lanes), 0)
    for j in range(GROUP):
        tile = step * GROUP + j
        owner = dest[tile]
        live = row < count[tile]
        raw = products(nk_ref[j], q_refs[j][0])
        codes = code_ref[owner]
        totals, picks = [], []
        for i in range(codes.shape[0]):
            part = raw[:, i * lanes : (i + 1) * lanes]
            code = codes[i : i + 1, :]
            expo = jnp.where(live, jnp.exp2(part * log2_scale), 0.0)
            total = jnp.sum(expo, axis=0, keepdims=True)
            totals.append(jnp.where(code > -2, total, 0.0))
            picked = jnp.sum(jnp.where(row == code, part, 0.0), axis=0, keepdims=True)
            picks.append(picked * inv_temp)
        out_ref[owner] = jnp.concatenate(totals + picks, axis=0)


def grad_kernel(dest, count, nk_ref, *rest):
    q_refs, code_ref, scale_ref, out_ref = (
        rest[:GROUP],
        rest[GROUP],
        rest[GROUP + 1],
        rest[GROUP + 2],
    )
    rows = nk_ref.shape[1]
    lanes = code_ref.shape[2]
    step = pl.program_id(0)
    row = lax.broadcasted_iota(jnp.int32, (rows, lanes), 0)
    for j in range(GROUP):
        tile = step * GROUP + j
        owner = dest[tile]
        live = row < count[tile]
        raw = products(nk_ref[j], q_refs[j][0])
        codes = code_ref[owner]
        scales = jnp.where(codes > -2, scale_ref[owner], 0.0)
        weights = []
        for i in range(codes.shape[0]):
            part = raw[:, i * lanes : (i + 1) * lanes]
            expo = jnp.where(live, jnp.exp2(part * log2_scale), 0.0)
            target = jnp.where(row == codes[i : i + 1, :], 1.0, 0.0)
            weights.append((expo * scales[i : i + 1, :] - target).astype(jnp.bfloat16))
        grad = jnp.dot(
            jnp.concatenate(weights, axis=1), q_refs[j][0], preferred_element_type=jnp.float32
        )
        out_ref[j] = (grad * inv_temp).astype(jnp.bfloat16)


def query_spec(j, block):
    return pl.BlockSpec(block, lambda step, dest, count: (dest[step * GROUP + j], 0, 0))


def tile_call(kernel, dest, count, nk, queries, tables, out_shape, out_spec, name):
    tiles, rows, width = nk.shape
    devices, query_rows, _ = queries.shape
    key_spec = pl.BlockSpec((GROUP, rows, width), lambda step, dest, count: (step, 0, 0))
    table_specs = [
        pl.BlockSpec(t.shape, lambda step, dest, count: (0, 0, 0)) for t in tables
    ]
    return pl.pallas_call(
        kernel,
        grid_spec=pltpu.PrefetchScalarGridSpec(
            num_scalar_prefetch=2,
            grid=(tiles // GROUP,),
            in_specs=[key_spec]
            + [query_spec(j, (1, query_rows, width)) for j in range(GROUP)]
            + table_specs,
            out_specs=out_spec,
        ),
        out_shape=out_shape,
        compiler_params=pltpu.CompilerParams(vmem_limit_bytes=48 * 1024 * 1024),
        name=name,
    )(dest, count, nk, *([queries] * GROUP), *tables)


def shards(key_feats, query_feats, key_dest, key_scene, key_count, pos_tile, pos_row):
    tiles, rows, width = key_feats.shape
    query_tiles = query_feats.shape[0]
    devices = lax.axis_size("cam") * lax.axis_size("lidar")
    normq = unit_rows(query_feats).reshape(1, query_tiles * rows, width)
    queries = lax.all_gather(normq, AXES, axis=0, tiled=True)

    device_iota = jnp.arange(devices, dtype=jnp.int32)
    owned = key_dest[None, :] == device_iota[:, None]
    scene_out = jnp.sum(jnp.where(owned, key_scene[None, :] + 1, 0), axis=1)
    scene_in = exchange(scene_out.reshape(devices, 1, 1)).reshape(devices)
    pos_source = pos_tile // tiles
    hit = pos_source[None, :] == device_iota[:, None]
    query_scene = jnp.sum(jnp.where(hit, scene_in[:, None], 0), axis=0)
    same = scene_in[:, None] == query_scene[None, :]
    code = jnp.where(
        hit[:, :, None], pos_row[None, :, :], jnp.where(same[:, :, None], -1, -2)
    )
    code = exchange(code)

    nk = unit_rows(key_feats)
    step_block = lambda step, dest, count: (step, 0, 0)
    whole = lambda step, dest, count: (0, 0, 0)
    partial = tile_call(
        total_kernel,
        key_dest,
        key_count,
        nk,
        queries,
        [code],
        jax.ShapeDtypeStruct((devices, 2 * query_tiles, rows), jnp.float32),
        pl.BlockSpec((devices, 2 * query_tiles, rows), whole),
        "totals",
    )
    arrived = jnp.sum(exchange(partial), axis=0)
    total, picked = arrived[:query_tiles], arrived[query_tiles:]
    scale = exchange(jnp.broadcast_to((1.0 / total)[None], (devices, query_tiles, rows)))
    loss = jnp.log(total) - picked
    key_grad = tile_call(
        grad_kernel,
        key_dest,
        key_count,
        nk,
        queries,
        [code, scale],
        jax.ShapeDtypeStruct((tiles, rows, width), jnp.bfloat16),
        pl.BlockSpec((GROUP, rows, width), step_block),
        "grads",
    )
    return (loss, key_grad)


def solution(mesh):
    return jax.shard_map(
        shards,
        mesh=mesh,
        in_specs=(
            P(AXES, None, None),
            P(AXES, None, None),
            P(AXES),
            P(AXES),
            P(AXES),
            P(AXES),
            P(AXES, None),
        ),
        out_specs=(P(AXES, None), P(AXES, None, None)),
        check_vma=False,
    )
```

time: 327 us -> 208 us (0.64)
  waiting for transfers between devices: 195 us -> 80.7 us
  matrix products: 53.7 us -> 0 us
  Pallas kernels: 0 us -> 36.8 us
  blocking collectives: 0 us -> 36 us
  local copies, waits for them, and re-layouts: 36.5 us -> 5.17 us
  starting transfers between devices: 30.5 us -> 15.9 us
  between operations: 0.79 us -> 14.1 us
  other arithmetic: 9.36 us -> 17.7 us
    all_to_all x3 -> x2, waiting for transfers between devices: 195 us -> 12.2 us  [exchange(): return lax.all_to_all(x, AXES, split_axis=0, concat_axis=0, tiled=True)]
    all_gather x0 -> x1, waiting for transfers between devices: none -> 68.5 us  [shards(): queries = lax.all_gather(normq, AXES, axis=0, tiled=True)]
    dot_general x4 -> x0, matrix products: 53.7 us -> none  [the longest x1 23.2 us: one_block(): jnp.einsum('qk,qe->ke', weights, queries, preferred_element_type=jnp.floa...]
    pallas_call x0 -> x2, Pallas kernels: none -> 36.8 us  [tile_call(): pl.pallas_call(kernel, grid_spec=pltpu.PrefetchScalarGridSpec(num_scalar_...]
    all_to_all x0 -> x2, blocking collectives: none -> 36 us  [exchange(): return lax.all_to_all(x, AXES, split_axis=0, concat_axis=0, tiled=True)]
    unnamed x13 -> x8, local copies, waits for them, and re-layouts: 27.2 us -> 4.39 us
    all_to_all x3 -> x2, starting transfers between devices: 30.5 us -> 15.9 us  [exchange(): return lax.all_to_all(x, AXES, split_axis=0, concat_axis=0, tiled=True)]
    gather x1 -> x0, local copies, waits for them, and re-layouts: 8.48 us -> none  [one_block(): picked = jnp.take_along_axis(logits, column[:, None], axis=1)[:, 0]]
  transfers between devices with their start and end apart: 3 -> 3, of which waited for: 2 -> 3; matrix products, arithmetic and copies ran while one was open for 10% -> 7% of each run, Pallas kernels for 0% -> 0%
where the time goes in v1:
time: 208 us; the launch traced here: 206 us
  waiting for transfers between devices  80.7 us (39%)
  Pallas kernels  36.8 us (18%)
  blocking collectives  36 us (17%)
  other arithmetic  17.7 us (9%)
  starting transfers between devices  15.9 us (8%)
  between operations  14.1 us (7%)
  local copies, waits for them, and re-layouts  5.17 us (2%)
    all_gather x1, waiting for transfers between devices, shards(): queries = lax.all_gather(normq, AXES, axis=0, tiled=True)  68.5 us
    pallas_call x2, Pallas kernels, tile_call(): pl.pallas_call(kernel, grid_spec=pltpu.PrefetchScalarGridSpec(num_scalar_...  36.8 us
    all_to_all x2, blocking collectives, exchange(): return lax.all_to_all(x, AXES, split_axis=0, concat_axis=0, tiled=True)  36 us
    all_to_all x2, starting transfers between devices, exchange(): return lax.all_to_all(x, AXES, split_axis=0, concat_axis=0, tiled=True)  15.9 us
    all_to_all x2, waiting for transfers between devices, exchange(): return lax.all_to_all(x, AXES, split_axis=0, concat_axis=0, tiled=True)  12.2 us
    convert_element_type x2, other arithmetic, unit_rows(): return scaled.astype(jnp.bfloat16)  6.02 us
    reduce_sum x2, other arithmetic, unit_rows(): jnp.mean(xf * xf, axis=-1, keepdims=True) + eps  4.61 us
    unnamed x8, local copies, waits for them, and re-layouts  4.39 us
  transfers between devices with their start and end apart: 3, of which 3 were waited for; matrix products, arithmetic and copies ran while one was open for 7% of the time, Pallas kernels for 0%

profile of v1, /device:TPU:1, one launch (start us, length us, event | category | flops | bytes accessed | tf_op | source)
XLA Modules:
  0.0 206.4 jit_solution(2162425783545361966)
XLA Ops:
  7.2 1.1 fusion.3
  8.3 1.8 fusion.5
  10.2 0.7 broadcast_add_fusion
  10.8 0.7 select_reduce_fusion.1
  11.6 0.7 copy.11
  12.3 11.5 %all-to-all-start = ((s32[128,1,1]{2,1,0:T(1,128)}), s32[128,1,1]{2,1,0:T(1,128)S(1)}, u32[]{:S(2)}, u32[]{:S(2)}) async-start(s32[128,1,1]{2,1,0:T(1,128)} %copy.11), calls=%async_computation | async-start | bytes 131072 | tf_op jit(solution)/shard_map/all_to_all | solution.py:26
  23.8 0.7 and_select_fusion
  24.5 3.5 %fusion = f32[64,128]{1,0:T(8,128)S(1)} fusion(bf16[64,128,256]{2,1,0:T(8,128)(2,1)} %param.7), kind=kLoop, calls=%fused_computation.2 | loop fusion | flops 6283264 | bytes 4227072 | tf_op jit(solution)/shard_map/reduce_sum | solution.py:20
  28.0 5.3 %all-to-all-done = s32[128,1,1]{2,1,0:T(1,128)S(1)} async-done(((s32[128,1,1]{2,1,0:T(1,128)}), s32[128,1,1]{2,1,0:T(1,128)S(1)}, u32[]{:S(2)}, u32[]{:S(2)}) %all-to-all-start) | async-done | bytes 544 | tf_op jit(solution)/shard_map/all_to_all | solution.py:26
  33.4 2.3 %reduce = s32[128]{0:T(128)S(1)} reduce(s32[128,1,1]{2,1,0:T(1,128)S(1)} %all-to-all-done, s32[]{:T(128)} %constant.32.clone.1), dimensions={1,2}, to_apply=%all_to_all.12.reduce_sub_computation | reduce | bytes 1028 | tf_op jit(solution)/shard_map/all_to_all | solution.py:26
  35.7 0.1 select_reduce_fusion
  35.9 1.7 broadcast_select_fusion
  37.7 4.4 %all-to-all-start.1 = ((s32[128,4,128]{2,1,0:T(4,128)}), s32[128,4,128]{2,1,0:T(4,128)S(1)}, u32[]{:S(2)}, u32[]{:S(2)}) async-start(s32[128,4,128]{2,1,0:T(4,128)} %broadcast_select_fusion), calls=%async_computation.1 | async-start | bytes 524288 | tf_op jit(solution)/shard_map/all_to_all | solution.py:26
  42.1 4.2 %fusion.2.nk_ref = bf16[64,128,256]{2,1,0:T(8,128)(2,1)} fusion(bf16[64,128,256]{2,1,0:T(8,128)(2,1)} %param.7, f32[64,128]{1,0:T(8,128)S(1)} %add_rsqrt_fusion), kind=kLoop, calls=%fused_computation.4 | loop fusion | flops 8388608 | bytes 8421376 | tf_op jit(solution)/shard_map/convert_element_type | solution.py:22
  46.3 6.9 %all-to-all-done.1.rest_4_ = s32[128,4,128]{2,1,0:T(4,128)S(1)} async-done(((s32[128,4,128]{2,1,0:T(4,128)}), s32[128,4,128]{2,1,0:T(4,128)S(1)}, u32[]{:S(2)}, u32[]{:S(2)}) %all-to-all-start.1) | async-done | bytes 262176 | tf_op jit(solution)/shard_map/all_to_all | solution.py:26
  53.2 68.5 %all-gather.2.cloned.1.call-done.rest_0_.rest_1_.rest_2_.rest_3_ = bf16[128,512,256]{2,1,0:T(8,128)(2,1)} async-done(((bf16[1,512,256]{2,1,0:T(8,128)(2,1)}), bf16[128,512,256]{2,1,0:T(8,128)(2,1)}) %all-gather.2.cloned.1.call-update) | async-done | bytes 33554448 | tf_op jit(solution)/shard_map/all_gather | solution.py:126
  121.6 2.2 %copy-done = bf16[64,128,256]{2,1,0:T(8,128)(2,1)S(1)} copy-done((bf16[64,128,256]{2,1,0:T(8,128)(2,1)S(1)}, bf16[64,128,256]{2,1,0:T(8,128)(2,1)}, u32[]{:S(2)}) %copy-start) | copy-done | bytes 4194328
  123.8 15.9 %totals.1 = f32[128,8,128]{2,1,0:T(8,128)S(1)} custom-call(s32[64]{0:T(128)S(1)} %copy-done.2, s32[64]{0:T(128)S(1)} %copy-done.3, bf16[64,128,256]{2,1,0:T(8,128)(2,1)S(1)} %copy-done, bf16[128,512,256]{2,1,0:T(8,128)(2,1)} %all-gather.2.cloned.1.call-done.rest_0_.rest_1_.rest_2_.rest_3_, ...), custom_call_target="tpu_custom_call" | custom-call | tf_op jit(solution)/shard_map/totals/pallas_call | solution.py:105
  139.7 20.8 %all_to_all.20 = f32[128,8,128]{2,1,0:T(8,128)S(1)} all-to-all(f32[128,8,128]{2,1,0:T(8,128)S(1)} %totals.1), channel_id=1, replica_groups=mesh['cam'=32,'lidar'=4] {'cam','lidar'}, dimensions={0} | all-to-all | bytes 1048576 | tf_op jit(solution)/shard_map/all_to_all | solution.py:26
  160.5 0.1 reduce_sum.49
  160.7 0.6 slice_divide_fusion
  161.3 15.2 %all_to_all.21.rest_5_ = f32[128,4,128]{2,1,0:T(4,128)S(1)} all-to-all(f32[128,4,128]{2,1,0:T(4,128)S(1)} %broadcast_in_dim.79), channel_id=1, replica_groups=mesh['cam'=32,'lidar'=4] {'cam','lidar'}, dimensions={0} | all-to-all | bytes 524288 | tf_op jit(solution)/shard_map/all_to_all | solution.py:26
  176.5 2.2 %copy-done.1 = bf16[64,128,256]{2,1,0:T(8,128)(2,1)S(1)} copy-done((bf16[64,128,256]{2,1,0:T(8,128)(2,1)S(1)}, bf16[64,128,256]{2,1,0:T(8,128)(2,1)}, u32[]{:S(2)}) %copy-start.1) | copy-done | bytes 4194328
  178.7 20.9 %grads.1 = bf16[64,128,256]{2,1,0:T(8,128)(2,1)} custom-call(s32[64]{0:T(128)S(1)} %copy-done.2, s32[64]{0:T(128)S(1)} %copy-done.3, bf16[64,128,256]{2,1,0:T(8,128)(2,1)S(1)} %copy-done.1, bf16[128,512,256]{2,1,0:T(8,128)(2,1)} %all-gather.2.cloned.1.call-done.rest_0_.rest_1_.rest_2_.rest_3_, ...), custom_call_target="tpu_custom_call" | custom-call | tf_op jit(solution)/shard_map/grads/pallas_call | solution.py:105
  (13 shorter events, 0.2 us)
Async XLA Ops:
  7.2 114.5 %copy-start.2 = (s32[64]{0:T(128)S(1)}, s32[64]{0:T(128)}, u32[]{:S(2)}) copy-start(s32[64]{0:T(128)} %dest.3) | copy-start | bytes 772
  7.2 114.5 %copy-start.3 = (s32[64]{0:T(128)S(1)}, s32[64]{0:T(128)}, u32[]{:S(2)}) copy-start(s32[64]{0:T(128)} %count.3) | copy-start | bytes 772
  7.2 114.4 %all-gather.2.cloned.1.call-start = ((), (), s32[]{:S(2)}) async-start(), calls=%async_computation.4 | async-start | bytes 33816576 | tf_op jit(solution)/shard_map/all_gather | solution.py:126
  12.3 21.1 %all-to-all-start = ((s32[128,1,1]{2,1,0:T(1,128)}), s32[128,1,1]{2,1,0:T(1,128)S(1)}, u32[]{:S(2)}, u32[]{:S(2)}) async-start(s32[128,1,1]{2,1,0:T(1,128)} %copy.11), calls=%async_computation | async-start | bytes 131072 | tf_op jit(solution)/shard_map/all_to_all | solution.py:26
  37.7 15.5 %all-to-all-start.1 = ((s32[128,4,128]{2,1,0:T(4,128)}), s32[128,4,128]{2,1,0:T(4,128)S(1)}, u32[]{:S(2)}, u32[]{:S(2)}) async-start(s32[128,4,128]{2,1,0:T(4,128)} %broadcast_select_fusion), calls=%async_computation.1 | async-start | bytes 524288 | tf_op jit(solution)/shard_map/all_to_all | solution.py:26
  121.6 2.2 %copy-start = (bf16[64,128,256]{2,1,0:T(8,128)(2,1)S(1)}, bf16[64,128,256]{2,1,0:T(8,128)(2,1)}, u32[]{:S(2)}) copy-start(bf16[64,128,256]{2,1,0:T(8,128)(2,1)} %fusion.2.nk_ref) | copy-start | bytes 12582916
  176.5 2.2 %copy-start.1 = (bf16[64,128,256]{2,1,0:T(8,128)(2,1)S(1)}, bf16[64,128,256]{2,1,0:T(8,128)(2,1)}, u32[]{:S(2)}) copy-start(bf16[64,128,256]{2,1,0:T(8,128)(2,1)} %fusion.2.nk_ref) | copy-start | bytes 12582916
Sparse Core Ops, SparseCore 0:
  11.2 110.4 all-gather.1

commit v2 on v1

v2 whole, which is shorter than its diff:
```python
import functools
import math

import jax
import jax.numpy as jnp
from jax import lax
from jax.experimental import pallas as pl
from jax.experimental.pallas import tpu as pltpu
from jax.sharding import PartitionSpec as P

inv_temp = 1.0 / 0.07
log2_scale = inv_temp * math.log2(math.e)
eps = 1e-06
GROUP = 8
AHEAD = 3
AXES = ("cam", "lidar")


def unit_rows(x):
    xf = x.astype(jnp.float32)
    scaled = (
        xf * lax.rsqrt(jnp.mean(xf * xf, axis=-1, keepdims=True) + eps) / math.sqrt(x.shape[-1])
    )
    return scaled.astype(jnp.bfloat16)


def exchange(x):
    return lax.all_to_all(x, AXES, split_axis=0, concat_axis=0, tiled=True)


def products(keys, queries):
    return lax.dot_general(
        keys, queries, (((1,), (1,)), ((), ())), preferred_element_type=jnp.float32
    )


def fetcher(pair_query, nk_hbm, q_hbm, nk_buf, q_buf, nk_sem, q_sem):
    pltpu.make_async_copy(nk_hbm, nk_buf, nk_sem).start()

    def fetch(group, act):
        for j in range(GROUP):
            p = group * GROUP + j
            copy = pltpu.make_async_copy(q_hbm.at[pair_query[p]], q_buf.at[p], q_sem.at[p])
            act(copy)

    return fetch


def over_groups(pairs, fetch, first, body):
    groups = (pairs + (GROUP - 1)) // GROUP
    start = lambda copy: copy.start()
    for ahead in range(AHEAD):

        @pl.when(ahead < groups)
        def _():
            fetch(ahead, start)

    first()

    @pl.loop(0, groups)
    def _(group):
        @pl.when(group + AHEAD < groups)
        def _():
            fetch(group + AHEAD, start)

        fetch(group, lambda copy: copy.wait())
        for j in range(GROUP):
            body(group * GROUP + j)


def total_kernel(
    slots, pair_tile, pair_query, pair_out, pairs, count, nk_hbm, q_hbm, code_ref, out_ref,
    nk_buf, q_buf, nk_sem, q_sem,
):
    rows = nk_buf.shape[1]
    row = lax.broadcasted_iota(jnp.int32, (rows, code_ref.shape[1]), 0)
    fetch = fetcher(pair_query, nk_hbm, q_hbm, nk_buf, q_buf, nk_sem, q_sem)

    def first():
        out_ref[...] = jnp.zeros_like(out_ref)
        pltpu.make_async_copy(nk_hbm, nk_buf, nk_sem).wait()

    def body(p):
        tile = pair_tile[p]
        raw = products(nk_buf[tile], q_buf[p])
        code = code_ref[pl.ds(pair_query[p], 1), :]
        expo = jnp.where(row < count[tile], jnp.exp2(raw * log2_scale), 0.0)
        total = jnp.sum(expo, axis=0, keepdims=True)
        picked = jnp.sum(jnp.where(row == code, raw, 0.0), axis=0, keepdims=True)
        out_ref[pl.ds(pair_out[p], 1), :] = jnp.where(code > -2, total, 0.0)
        out_ref[pl.ds(pair_out[p] + slots, 1), :] = picked * inv_temp

    over_groups(pairs[0], fetch, first, body)


def grad_kernel(
    pair_tile, pair_query, pairs, count, nk_hbm, q_hbm, code_ref, scale_ref, out_hbm,
    nk_buf, q_buf, sum_buf, out_buf, nk_sem, q_sem, out_sem,
):
    tiles, rows, width = nk_buf.shape
    row = lax.broadcasted_iota(jnp.int32, (rows, code_ref.shape[1]), 0)
    grad_row = lax.broadcasted_iota(jnp.int32, (rows, width), 0)
    fetch = fetcher(pair_query, nk_hbm, q_hbm, nk_buf, q_buf, nk_sem, q_sem)

    def first():
        sum_buf[...] = jnp.zeros_like(sum_buf)
        pltpu.make_async_copy(nk_hbm, nk_buf, nk_sem).wait()

    def body(p):
        tile, query = pair_tile[p], pair_query[p]
        raw = products(nk_buf[tile], q_buf[p])
        code = jnp.where(p < pairs[0], code_ref[pl.ds(query, 1), :], -2)
        scale = jnp.where(code > -2, scale_ref[pl.ds(query, 1), :], 0.0)
        target = jnp.where(row == code, 1.0, 0.0)
        weights = (jnp.exp2(raw * log2_scale) * scale - target).astype(jnp.bfloat16)
        sum_buf[tile] += jnp.dot(weights, q_buf[p], preferred_element_type=jnp.float32)

    over_groups(pairs[0], fetch, first, body)

    def part(group):
        span = pl.ds(group * GROUP, GROUP)
        return pltpu.make_async_copy(out_buf.at[span], out_hbm.at[span], out_sem.at[group])

    @pl.loop(0, tiles // GROUP)
    def _(group):
        for j in range(GROUP):
            tile = group * GROUP + j
            grad = jnp.where(grad_row < count[tile], sum_buf[tile] * inv_temp, 0.0)
            out_buf[tile] = grad.astype(jnp.bfloat16)
        part(group).start()

    @pl.loop(0, tiles // GROUP)
    def _(group):
        part(group).wait()


def tile_call(kernel, scalars, nk, queries, tables, out_shape, wide, name):
    tiles, rows, width = nk.shape
    most = scalars[0].shape[0]
    query_rows = queries.shape[1]
    smem, vmem, hbm = (pl.BlockSpec(memory_space=m) for m in (pltpu.SMEM, pltpu.VMEM, pl.ANY))
    buffers = [
        pltpu.VMEM((tiles, rows, width), jnp.bfloat16),
        pltpu.VMEM((most, query_rows, width), jnp.bfloat16),
    ]
    semaphores = [pltpu.SemaphoreType.DMA, pltpu.SemaphoreType.DMA((most,))]
    if wide:
        buffers += [
            pltpu.VMEM((tiles, rows, width), jnp.float32),
            pltpu.VMEM((tiles, rows, width), jnp.bfloat16),
        ]
        semaphores += [pltpu.SemaphoreType.DMA((tiles // GROUP,))]
    return pl.pallas_call(
        kernel,
        in_specs=[smem] * len(scalars) + [hbm, hbm] + [vmem] * len(tables),
        out_specs=hbm if wide else vmem,
        out_shape=out_shape,
        scratch_shapes=buffers + semaphores,
        compiler_params=pltpu.CompilerParams(vmem_limit_bytes=58 * 1024 * 1024),
        name=name,
    )(*scalars, nk, queries, *tables)


def pair_lists(code, key_dest, query_tiles):
    devices = code.shape[0]
    most = key_dest.shape[0] * query_tiles
    owned = key_dest[:, None] == jnp.arange(devices, dtype=jnp.int32)[None, :]
    allowed = (code[:, :, 0] > -2).astype(jnp.int32)
    match = jnp.sum(jnp.where(owned[:, :, None], allowed[None], 0), axis=1).reshape(most)
    index = jnp.arange(most, dtype=jnp.int32)
    place = jnp.sum(jnp.where(index[None, :] < index[:, None], match[None, :], 0), axis=1)
    tile = index // query_tiles
    slot = index % query_tiles
    owner = jnp.repeat(key_dest, query_tiles)
    chosen = (place[None, :] == index[:, None]) & (match[None, :] > 0)
    listed = lambda x: jnp.sum(jnp.where(chosen, x[None, :], 0), axis=1)
    pairs = jnp.sum(match)
    spare = index >= pairs
    pair_tile = listed(tile)
    pair_query = jnp.where(spare, owner[0] * query_tiles, listed(owner * query_tiles + slot))
    pair_out = jnp.where(
        spare, owner[0] * 2 * query_tiles, listed(owner * 2 * query_tiles + slot)
    )
    return pair_tile, pair_query, pair_out, pairs.reshape(1)


def shards(key_feats, query_feats, key_dest, key_scene, key_count, pos_tile, pos_row):
    tiles, rows, width = key_feats.shape
    query_tiles = query_feats.shape[0]
    devices = lax.axis_size("cam") * lax.axis_size("lidar")
    queries = lax.all_gather(unit_rows(query_feats), AXES, axis=0, tiled=True)

    device_iota = jnp.arange(devices, dtype=jnp.int32)
    owned = key_dest[None, :] == device_iota[:, None]
    scene_out = jnp.sum(jnp.where(owned, key_scene[None, :] + 1, 0), axis=1)
    scene_in = exchange(scene_out.reshape(devices, 1, 1)).reshape(devices)
    pos_source = pos_tile // tiles
    hit = pos_source[None, :] == device_iota[:, None]
    query_scene = jnp.sum(jnp.where(hit, scene_in[:, None], 0), axis=0)
    same = scene_in[:, None] == query_scene[None, :]
    code = jnp.where(
        hit[:, :, None], pos_row[None, :, :], jnp.where(same[:, :, None], -1, -2)
    )
    code = exchange(code)

    nk = unit_rows(key_feats)
    pair_tile, pair_query, pair_out, pairs = pair_lists(code, key_dest, query_tiles)
    code = code.reshape(devices * query_tiles, rows)
    partial = tile_call(
        functools.partial(total_kernel, query_tiles),
        [pair_tile, pair_query, pair_out, pairs, key_count],
        nk,
        queries,
        [code],
        jax.ShapeDtypeStruct((devices * 2 * query_tiles, rows), jnp.float32),
        False,
        "totals",
    )
    partial = partial.reshape(devices, 2 * query_tiles, rows)
    arrived = jnp.sum(exchange(partial), axis=0)
    total, picked = arrived[:query_tiles], arrived[query_tiles:]
    scale = exchange(jnp.broadcast_to((1.0 / total)[None], (devices, query_tiles, rows)))
    loss = jnp.log(total) - picked
    key_grad = tile_call(
        grad_kernel,
        [pair_tile, pair_query, pairs, key_count],
        nk,
        queries,
        [code, scale.reshape(devices * query_tiles, rows)],
        jax.ShapeDtypeStruct((tiles, rows, width), jnp.bfloat16),
        True,
        "grads",
    )
    return (loss, key_grad)


def solution(mesh):
    return jax.shard_map(
        shards,
        mesh=mesh,
        in_specs=(
            P(AXES, None, None),
            P(AXES, None, None),
            P(AXES),
            P(AXES),
            P(AXES),
            P(AXES),
            P(AXES, None),
        ),
        out_specs=(P(AXES, None), P(AXES, None, None)),
        check_vma=False,
    )
```

time: 208 us -> 195 us (0.938)
  Pallas kernels: 36.8 us -> 24.9 us
  waiting for transfers between devices: 80.7 us -> 73.1 us
  starting transfers between devices: 15.9 us -> 21 us
  local copies, waits for them, and re-layouts: 5.17 us -> 2.44 us
  other arithmetic: 17.7 us -> 19.9 us
    pallas_call x2, Pallas kernels: 36.8 us -> 24.9 us  [tile_call(): pl.pallas_call(kernel, in_specs=[smem] * len(scalars) + [hbm, hbm] + [vme...]
    all_gather x1, waiting for transfers between devices: 68.5 us -> 62.6 us  [shards(): queries = lax.all_gather(unit_rows(query_feats), AXES, axis=0, tiled=True)]
    all_to_all x2, starting transfers between devices: 15.9 us -> 20.9 us  [exchange(): return lax.all_to_all(x, AXES, split_axis=0, concat_axis=0, tiled=True)]
    unnamed x8 -> x7, local copies, waits for them, and re-layouts: 4.39 us -> 0.11 us
  transfers between devices with their start and end apart: 3 -> 3, of which waited for: 3 -> 3; matrix products, arithmetic and copies ran while one was open for 7% -> 10% of each run, Pallas kernels for 0% -> 0%
where the time goes in v2:
time: 195 us; the launch traced here: 194 us
  waiting for transfers between devices  73.1 us (37%)
  blocking collectives  36.9 us (19%)
  Pallas kernels  24.9 us (13%)
  starting transfers between devices  21 us (11%)
  other arithmetic  19.9 us (10%)
  between operations  15.5 us (8%)
  local copies, waits for them, and re-layouts  2.44 us (1%)
    all_gather x1, waiting for transfers between devices, shards(): queries = lax.all_gather(unit_rows(query_feats), AXES, axis=0, tiled=True)  62.6 us
    all_to_all x2, blocking collectives, exchange(): return lax.all_to_all(x, AXES, split_axis=0, concat_axis=0, tiled=True)  36.9 us
    pallas_call x2, Pallas kernels, tile_call(): pl.pallas_call(kernel, in_specs=[smem] * len(scalars) + [hbm, hbm] + [vme...  24.9 us
    all_to_all x2, starting transfers between devices, exchange(): return lax.all_to_all(x, AXES, split_axis=0, concat_axis=0, tiled=True)  20.9 us
    all_to_all x2, waiting for transfers between devices, exchange(): return lax.all_to_all(x, AXES, split_axis=0, concat_axis=0, tiled=True)  10.5 us
    convert_element_type x2, other arithmetic, unit_rows(): return scaled.astype(jnp.bfloat16)  6.07 us
    reduce_sum x2, other arithmetic, unit_rows(): jnp.mean(xf * xf, axis=-1, keepdims=True) + eps  4.52 us
  transfers between devices with their start and end apart: 3, of which 3 were waited for; matrix products, arithmetic and copies ran while one was open for 10% of the time, Pallas kernels for 0%

profile of v2, /device:TPU:1, one launch (start us, length us, event | category | flops | bytes accessed | tf_op | source)
XLA Modules:
  0.0 193.7 jit_solution(13932034871647303567)
XLA Ops:
  7.2 1.1 fusion.3
  8.3 1.8 fusion.5
  10.2 0.7 broadcast_add_fusion
  10.8 0.7 select_reduce_fusion.7
  11.6 0.7 copy.28
  12.3 11.5 %all-to-all-start = ((s32[128,1,1]{2,1,0:T(1,128)}), s32[128,1,1]{2,1,0:T(1,128)S(1)}, u32[]{:S(2)}, u32[]{:S(2)}) async-start(s32[128,1,1]{2,1,0:T(1,128)} %copy.28), calls=%async_computation | async-start | bytes 131072 | tf_op jit(solution)/shard_map/all_to_all | solution.py:28
  23.8 0.7 broadcast_in_dim.162
  24.7 0.7 and_select_fusion.2
  25.4 3.4 %fusion = f32[64,128]{1,0:T(8,128)S(1)} fusion(bf16[64,128,256]{2,1,0:T(8,128)(2,1)} %param.7), kind=kLoop, calls=%fused_computation.2 | loop fusion | flops 6283264 | bytes 4227072 | tf_op jit(solution)/shard_map/reduce_sum | solution.py:22
  28.8 4.3 %fusion.2.nk_hbm = bf16[64,128,256]{2,1,0:T(8,128)(2,1)} fusion(bf16[64,128,256]{2,1,0:T(8,128)(2,1)} %param.7, f32[64,128]{1,0:T(8,128)S(1)} %add_rsqrt_fusion), kind=kLoop, calls=%fused_computation.4 | loop fusion | flops 8388608 | bytes 8421376 | tf_op jit(solution)/shard_map/convert_element_type | solution.py:24
  33.4 2.3 %reduce.2 = s32[128]{0:T(128)S(1)} reduce(s32[128,1,1]{2,1,0:T(1,128)S(1)} %all-to-all-done, s32[]{:T(128)} %constant.62.clone.1), dimensions={1,2}, to_apply=%all_to_all.12.reduce_sub_computation | reduce | bytes 1028 | tf_op jit(solution)/shard_map/all_to_all | solution.py:28
  36.0 1.0 broadcast_select_fusion
  37.0 9.4 %all-to-all-start.1 = ((s32[128,4,128]{2,1,0:T(4,128)}), s32[128,4,128]{2,1,0:T(4,128)S(1)}, u32[]{:S(2)}, u32[]{:S(2)}) async-start(s32[128,4,128]{2,1,0:T(4,128)} %broadcast_select_fusion), calls=%async_computation.1 | async-start | bytes 524288 | tf_op jit(solution)/shard_map/all_to_all | solution.py:28
  46.5 0.5 slice.14
  48.3 10.2 %all-to-all-done.1 = s32[128,4,128]{2,1,0:T(4,128)S(1)} async-done(((s32[128,4,128]{2,1,0:T(4,128)}), s32[128,4,128]{2,1,0:T(4,128)S(1)}, u32[]{:S(2)}, u32[]{:S(2)}) %all-to-all-start.1) | async-done | bytes 262176 | tf_op jit(solution)/shard_map/all_to_all | solution.py:28
  58.7 0.7 select_reduce_fusion.4
  59.7 0.8 select_reduce_fusion
  60.5 1.2 fusion.9
  61.7 62.6 %all-gather.2.cloned.1.call-done.q_hbm = bf16[512,128,256]{2,1,0:T(8,128)(2,1)} async-done(((bf16[4,128,256]{2,1,0:T(8,128)(2,1)}), bf16[512,128,256]{2,1,0:T(8,128)(2,1)}) %all-gather.2.cloned.1.call-update) | async-done | bytes 33554448 | tf_op jit(solution)/shard_map/all_gather | solution.py:191
  124.3 10.3 %totals.1 = f32[1024,128]{1,0:T(8,128)} custom-call(s32[256]{0:T(256)} %get-tuple-element.6.pair_tile, s32[256]{0:T(256)} %get-tuple-element.12.pair_query, s32[256]{0:T(256)} %get-tuple-element.11.pair_out, s32[1]{0:T(128)} %bitcast.4.pairs, s32[64]{0:T(128)} %count.3, bf16[64,128,256]{2,1,0:T(8,128)(2,1)} %fusion.2.nk_hbm, ...), custom_call_target="tpu_custom_call" | custom-call | tf_op jit(solution)/shard_map/totals/pallas_call | solution.py:153
  134.6 21.6 %all_to_all.20 = f32[128,8,128]{2,1,0:T(8,128)S(1)} all-to-all(f32[128,8,128]{2,1,0:T(8,128)} %bitcast.13), channel_id=1, replica_groups=mesh['cam'=32,'lidar'=4] {'cam','lidar'}, dimensions={0} | all-to-all | bytes 1048576 | tf_op jit(solution)/shard_map/all_to_all | solution.py:28
  156.3 0.6 slice_divide_fusion
  157.0 15.3 %all_to_all.21 = f32[128,4,128]{2,1,0:T(4,128)} all-to-all(f32[128,4,128]{2,1,0:T(4,128)S(1)} %broadcast_in_dim.167), channel_id=1, replica_groups=mesh['cam'=32,'lidar'=4] {'cam','lidar'}, dimensions={0} | all-to-all | bytes 524288 | tf_op jit(solution)/shard_map/all_to_all | solution.py:28
  172.3 14.6 %grads.1 = bf16[64,128,256]{2,1,0:T(8,128)(2,1)} custom-call(s32[256]{0:T(256)} %get-tuple-element.6.pair_tile, s32[256]{0:T(256)} %get-tuple-element.12.pair_query, s32[1]{0:T(128)} %bitcast.4.pairs, s32[64]{0:T(128)} %count.3, bf16[64,128,256]{2,1,0:T(8,128)(2,1)} %fusion.2.nk_hbm, bf16[512,128,256]{2,1,0:T(8,128)(2,1)} %all-gather.2.cloned.1.call-done.q_hbm, ...), custom_call_target="tpu_custom_call" | custom-call | tf_op jit(solution)/shard_map/grads/pallas_call | solution.py:153
  (26 shorter events, 1.4 us)
Async XLA Ops:
  7.2 41.1 %copy-start.2 = (s32[64]{0:T(128)S(1)}, s32[64]{0:T(128)}, u32[]{:S(2)}) copy-start(s32[64]{0:T(128)} %param.9) | copy-start | bytes 772
  7.2 28.8 %copy-start.1 = (s32[4,128]{1,0:T(4,128)S(1)}, s32[4,128]{1,0:T(4,128)}, u32[]{:S(2)}) copy-start(s32[4,128]{1,0:T(4,128)} %param.13) | copy-start | bytes 6148
  7.2 117.1 %all-gather.2.cloned.1.call-start = ((), (), s32[]{:S(2)}) async-start(), calls=%async_computation.4 | async-start | bytes 33816576 | tf_op jit(solution)/shard_map/all_gather | solution.py:191
  12.3 21.1 %all-to-all-start = ((s32[128,1,1]{2,1,0:T(1,128)}), s32[128,1,1]{2,1,0:T(1,128)S(1)}, u32[]{:S(2)}, u32[]{:S(2)}) async-start(s32[128,1,1]{2,1,0:T(1,128)} %copy.28), calls=%async_computation | async-start | bytes 131072 | tf_op jit(solution)/shard_map/all_to_all | solution.py:28
  37.0 21.6 %all-to-all-start.1 = ((s32[128,4,128]{2,1,0:T(4,128)}), s32[128,4,128]{2,1,0:T(4,128)S(1)}, u32[]{:S(2)}, u32[]{:S(2)}) async-start(s32[128,4,128]{2,1,0:T(4,128)} %broadcast_select_fusion), calls=%async_computation.1 | async-start | bytes 524288 | tf_op jit(solution)/shard_map/all_to_all | solution.py:28
  58.6 65.7 %copy-start = (s32[128,4,128]{2,1,0:T(4,128)}, s32[128,4,128]{2,1,0:T(4,128)S(1)}, u32[]{:S(2)}) copy-start(s32[128,4,128]{2,1,0:T(4,128)S(1)} %all-to-all-done.1) | copy-start | bytes 786436
Sparse Core Ops, SparseCore 0:
  11.2 113.0 all-gather.1

commit v3 on v2

--- a/solution.py
+++ b/solution.py
@@ -11,8 +11,9 @@
 inv_temp = 1.0 / 0.07
 log2_scale = inv_temp * math.log2(math.e)
 eps = 1e-06
-GROUP = 8
-AHEAD = 3
+TOTAL_GROUP = 8
+GRAD_GROUP = 16
+OUT_GROUP = 8
 AXES = ("cam", "lidar")
 
 
@@ -34,128 +35,124 @@
     )
 
 
-def fetcher(pair_query, nk_hbm, q_hbm, nk_buf, q_buf, nk_sem, q_sem):
-    pltpu.make_async_copy(nk_hbm, nk_buf, nk_sem).start()
-
-    def fetch(group, act):
-        for j in range(GROUP):
-            p = group * GROUP + j
-            copy = pltpu.make_async_copy(q_hbm.at[pair_query[p]], q_buf.at[p], q_sem.at[p])
-            act(copy)
-
-    return fetch
-
-
-def over_groups(pairs, fetch, first, body):
-    groups = (pairs + (GROUP - 1)) // GROUP
+def over_pairs(pairs, group, sources, first, body):
+    slots = sources[0][2].shape[0]
+    ahead = slots // group - 1
+    groups = (pairs + (group - 1)) // group
+
+    def fetch(step, act):
+        base = lax.rem(step, ahead + 1) * group
+        for j in range(group):
+            for hbm, index, buf, sem in sources:
+                copy = pltpu.make_async_copy(
+                    hbm.at[index[step * group + j]], buf.at[base + j], sem.at[base + j]
+                )
+                act(copy)
+
     start = lambda copy: copy.start()
-    for ahead in range(AHEAD):
-
-        @pl.when(ahead < groups)
+    for early in range(ahead):
+
+        @pl.when(early < groups)
         def _():
-            fetch(ahead, start)
+            fetch(early, start)
 
     first()
 
     @pl.loop(0, groups)
-    def _(group):
-        @pl.when(group + AHEAD < groups)
+    def _(step):
+        @pl.when(step + ahead < groups)
         def _():
-            fetch(group + AHEAD, start)
-
-        fetch(group, lambda copy: copy.wait())
-        for j in range(GROUP):
-            body(group * GROUP + j)
+            fetch(step + ahead, start)
+
+        fetch(step, lambda copy: copy.wait())
+        base = lax.rem(step, ahead + 1) * group
+        for j in range(group):
+            body(step * group + j, base + j)
 
 
 def total_kernel(
     slots, pair_tile, pair_query, pair_out, pairs, count, nk_hbm, q_hbm, code_ref, out_ref,
     nk_buf, q_buf, nk_sem, q_sem,
 ):
-    rows = nk_buf.shape[1]
-    row = lax.broadcasted_iota(jnp.int32, (rows, code_ref.shape[1]), 0)
-    fetch = fetcher(pair_query, nk_hbm, q_hbm, nk_buf, q_buf, nk_sem, q_sem)
+    row = lax.broadcasted_iota(jnp.int32, (nk_buf.shape[1], code_ref.shape[1]), 0)
 
     def first():
         out_ref[...] = jnp.zeros_like(out_ref)
-        pltpu.make_async_copy(nk_hbm, nk_buf, nk_sem).wait()
-
-    def body(p):
-        tile = pair_tile[p]
-        raw = products(nk_buf[tile], q_buf[p])
+
+    def body(p, slot):
+        raw = products(nk_buf[slot], q_buf[slot])
         code = code_ref[pl.ds(pair_query[p], 1), :]
-        expo = jnp.where(row < count[tile], jnp.exp2(raw * log2_scale), 0.0)
+        expo = jnp.where(row < count[pair_tile[p]], jnp.exp2(raw * log2_scale), 0.0)
         total = jnp.sum(expo, axis=0, keepdims=True)
         picked = jnp.sum(jnp.where(row == code, raw, 0.0), axis=0, keepdims=True)
         out_ref[pl.ds(pair_out[p], 1), :] = jnp.where(code > -2, total, 0.0)
         out_ref[pl.ds(pair_out[p] + slots, 1), :] = picked * inv_temp
 
-    over_groups(pairs[0], fetch, first, body)
+    sources = [(nk_hbm, pair_tile, nk_buf, nk_sem), (q_hbm, pair_query, q_buf, q_sem)]
+    over_pairs(pairs[0], TOTAL_GROUP, sources, first, body)
 
 
 def grad_kernel(
     pair_tile, pair_query, pairs, count, nk_hbm, q_hbm, code_ref, scale_ref, out_hbm,
-    nk_buf, q_buf, sum_buf, out_buf, nk_sem, q_sem, out_sem,
+    nk_buf, q_buf, nk_sem, q_sem, sum_buf, out_buf, out_sem,
 ):
-    tiles, rows, width = nk_buf.shape
+    tiles, rows, width = sum_buf.shape
     row = lax.broadcasted_iota(jnp.int32, (rows, code_ref.shape[1]), 0)
     grad_row = lax.broadcasted_iota(jnp.int32, (rows, width), 0)
-    fetch = fetcher(pair_query, nk_hbm, q_hbm, nk_buf, q_buf, nk_sem, q_sem)
 
     def first():
         sum_buf[...] = jnp.zeros_like(sum_buf)
-        pltpu.make_async_copy(nk_hbm, nk_buf, nk_sem).wait()
-
-    def body(p):
+
+    def body(p, slot):
         tile, query = pair_tile[p], pair_query[p]
-        raw = products(nk_buf[tile], q_buf[p])
+        raw = products(nk_buf[slot], q_buf[slot])
         code = jnp.where(p < pairs[0], code_ref[pl.ds(query, 1), :], -2)
         scale = jnp.where(code > -2, scale_ref[pl.ds(query, 1), :], 0.0)
         target = jnp.where(row == code, 1.0, 0.0)
         weights = (jnp.exp2(raw * log2_scale) * scale - target).astype(jnp.bfloat16)
-        sum_buf[tile] += jnp.dot(weights, q_buf[p], preferred_element_type=jnp.float32)
-
-    over_groups(pairs[0], fetch, first, body)
+        sum_buf[tile] += jnp.dot(weights, q_buf[slot], preferred_element_type=jnp.float32)
+
+    sources = [(nk_hbm, pair_tile, nk_buf, nk_sem), (q_hbm, pair_query, q_buf, q_sem)]
+    over_pairs(pairs[0], GRAD_GROUP, sources, first, body)
 
     def part(group):
-        span = pl.ds(group * GROUP, GROUP)
+        span = pl.ds(group * OUT_GROUP, OUT_GROUP)
         return pltpu.make_async_copy(out_buf.at[span], out_hbm.at[span], out_sem.at[group])
 
-    @pl.loop(0, tiles // GROUP)
+    @pl.loop(0, tiles // OUT_GROUP)
     def _(group):
-        for j in range(GROUP):
-            tile = group * GROUP + j
+        for j in range(OUT_GROUP):
+            tile = group * OUT_GROUP + j
             grad = jnp.where(grad_row < count[tile], sum_buf[tile] * inv_temp, 0.0)
             out_buf[tile] = grad.astype(jnp.bfloat16)
         part(group).start()
 
-    @pl.loop(0, tiles // GROUP)
+    @pl.loop(0, tiles // OUT_GROUP)
     def _(group):
         part(group).wait()
 
 
-def tile_call(kernel, scalars, nk, queries, tables, out_shape, wide, name):
+def tile_call(kernel, scalars, nk, queries, tables, out_shape, slots, wide, name):
     tiles, rows, width = nk.shape
-    most = scalars[0].shape[0]
-    query_rows = queries.shape[1]
     smem, vmem, hbm = (pl.BlockSpec(memory_space=m) for m in (pltpu.SMEM, pltpu.VMEM, pl.ANY))
-    buffers = [
-        pltpu.VMEM((tiles, rows, width), jnp.bfloat16),
-        pltpu.VMEM((most, query_rows, width), jnp.bfloat16),
+    scratch = [
+        pltpu.VMEM((slots, rows, width), jnp.bfloat16),
+        pltpu.VMEM((slots,) + queries.shape[1:], jnp.bfloat16),
+        pltpu.SemaphoreType.DMA((slots,)),
+        pltpu.SemaphoreType.DMA((slots,)),
     ]
-    semaphores = [pltpu.SemaphoreType.DMA, pltpu.SemaphoreType.DMA((most,))]
     if wide:
-        buffers += [
+        scratch += [
             pltpu.VMEM((tiles, rows, width), jnp.float32),
             pltpu.VMEM((tiles, rows, width), jnp.bfloat16),
+            pltpu.SemaphoreType.DMA((tiles // OUT_GROUP,)),
         ]
-        semaphores += [pltpu.SemaphoreType.DMA((tiles // GROUP,))]
     return pl.pallas_call(
         kernel,
         in_specs=[smem] * len(scalars) + [hbm, hbm] + [vmem] * len(tables),
         out_specs=hbm if wide else vmem,
         out_shape=out_shape,
-        scratch_shapes=buffers + semaphores,
+        scratch_shapes=scratch,
         compiler_params=pltpu.CompilerParams(vmem_limit_bytes=58 * 1024 * 1024),
         name=name,
     )(*scalars, nk, queries, *tables)
@@ -213,6 +210,7 @@
         queries,
         [code],
         jax.ShapeDtypeStruct((devices * 2 * query_tiles, rows), jnp.float32),
+        4 * TOTAL_GROUP,
         False,
         "totals",
     )
@@ -228,6 +226,7 @@
         queries,
         [code, scale.reshape(devices * query_tiles, rows)],
         jax.ShapeDtypeStruct((tiles, rows, width), jnp.bfloat16),
+        3 * GRAD_GROUP,
         True,
         "grads",
     )

time: 195 us -> 190 us (0.974)
  Pallas kernels: 24.9 us -> 16.8 us
    pallas_call x2, Pallas kernels: 24.9 us -> 16.8 us  [tile_call(): pl.pallas_call(kernel, in_specs=[smem] * len(scalars) + [hbm, hbm] + [vme...]
where the time goes in v3:
time: 190 us; the launch traced here: 187 us
  waiting for transfers between devices  73.1 us (38%)
  blocking collectives  38.4 us (20%)
  starting transfers between devices  21 us (11%)
  other arithmetic  19.9 us (10%)
  Pallas kernels  16.8 us (9%)
  between operations  15.5 us (8%)
  local copies, waits for them, and re-layouts  2.44 us (1%)
    all_gather x1, waiting for transfers between devices, shards(): queries = lax.all_gather(unit_rows(query_feats), AXES, axis=0, tiled=True)  62.6 us
    all_to_all x2, blocking collectives, exchange(): return lax.all_to_all(x, AXES, split_axis=0, concat_axis=0, tiled=True)  38.4 us
    all_to_all x2, starting transfers between devices, exchange(): return lax.all_to_all(x, AXES, split_axis=0, concat_axis=0, tiled=True)  20.9 us
    pallas_call x2, Pallas kernels, tile_call(): pl.pallas_call(kernel, in_specs=[smem] * len(scalars) + [hbm, hbm] + [vme...  16.8 us
    all_to_all x2, waiting for transfers between devices, exchange(): return lax.all_to_all(x, AXES, split_axis=0, concat_axis=0, tiled=True)  10.5 us
    convert_element_type x2, other arithmetic, unit_rows(): return scaled.astype(jnp.bfloat16)  6.07 us
    reduce_sum x2, other arithmetic, unit_rows(): jnp.mean(xf * xf, axis=-1, keepdims=True) + eps  4.52 us
  transfers between devices with their start and end apart: 3, of which 3 were waited for; matrix products, arithmetic and copies ran while one was open for 10% of the time, Pallas kernels for 0%

profile of v3, /device:TPU:1, one launch (start us, length us, event | category | flops | bytes accessed | tf_op | source)
XLA Modules:
  0.0 187.0 jit_solution(12731359171139571600)
XLA Ops:
  7.2 1.1 fusion.3
  8.3 1.8 fusion.5
  10.2 0.7 broadcast_add_fusion
  10.8 0.7 select_reduce_fusion.7
  11.6 0.7 copy.28
  12.3 11.5 %all-to-all-start = ((s32[128,1,1]{2,1,0:T(1,128)}), s32[128,1,1]{2,1,0:T(1,128)S(1)}, u32[]{:S(2)}, u32[]{:S(2)}) async-start(s32[128,1,1]{2,1,0:T(1,128)} %copy.28), calls=%async_computation | async-start | bytes 131072 | tf_op jit(solution)/shard_map/all_to_all | solution.py:29
  23.8 0.7 broadcast_in_dim.162
  24.7 0.7 and_select_fusion.2
  25.4 3.4 %fusion = f32[64,128]{1,0:T(8,128)S(1)} fusion(bf16[64,128,256]{2,1,0:T(8,128)(2,1)} %param.7), kind=kLoop, calls=%fused_computation.2 | loop fusion | flops 6283264 | bytes 4227072 | tf_op jit(solution)/shard_map/reduce_sum | solution.py:23
  28.8 4.3 %fusion.2.nk_hbm = bf16[64,128,256]{2,1,0:T(8,128)(2,1)} fusion(bf16[64,128,256]{2,1,0:T(8,128)(2,1)} %param.7, f32[64,128]{1,0:T(8,128)S(1)} %add_rsqrt_fusion), kind=kLoop, calls=%fused_computation.4 | loop fusion | flops 8388608 | bytes 8421376 | tf_op jit(solution)/shard_map/convert_element_type | solution.py:25
  33.4 2.3 %reduce.2 = s32[128]{0:T(128)S(1)} reduce(s32[128,1,1]{2,1,0:T(1,128)S(1)} %all-to-all-done, s32[]{:T(128)} %constant.62.clone.1), dimensions={1,2}, to_apply=%all_to_all.12.reduce_sub_computation | reduce | bytes 1028 | tf_op jit(solution)/shard_map/all_to_all | solution.py:29
  36.0 1.0 broadcast_select_fusion
  37.0 9.4 %all-to-all-start.1 = ((s32[128,4,128]{2,1,0:T(4,128)}), s32[128,4,128]{2,1,0:T(4,128)S(1)}, u32[]{:S(2)}, u32[]{:S(2)}) async-start(s32[128,4,128]{2,1,0:T(4,128)} %broadcast_select_fusion), calls=%async_computation.1 | async-start | bytes 524288 | tf_op jit(solution)/shard_map/all_to_all | solution.py:29
  46.5 0.5 slice.14
  48.3 10.2 %all-to-all-done.1 = s32[128,4,128]{2,1,0:T(4,128)S(1)} async-done(((s32[128,4,128]{2,1,0:T(4,128)}), s32[128,4,128]{2,1,0:T(4,128)S(1)}, u32[]{:S(2)}, u32[]{:S(2)}) %all-to-all-start.1) | async-done | bytes 262176 | tf_op jit(solution)/shard_map/all_to_all | solution.py:29
  58.7 0.7 select_reduce_fusion.4
  59.7 0.8 select_reduce_fusion
  60.5 1.2 fusion.9
  61.7 62.6 %all-gather.2.cloned.1.call-done.q_hbm = bf16[512,128,256]{2,1,0:T(8,128)(2,1)} async-done(((bf16[4,128,256]{2,1,0:T(8,128)(2,1)}), bf16[512,128,256]{2,1,0:T(8,128)(2,1)}) %all-gather.2.cloned.1.call-update) | async-done | bytes 33554448 | tf_op jit(solution)/shard_map/all_gather | solution.py:188
  124.3 7.0 %totals.1 = f32[1024,128]{1,0:T(8,128)} custom-call(s32[256]{0:T(256)} %get-tuple-element.6.pair_tile, s32[256]{0:T(256)} %get-tuple-element.12.pair_query, s32[256]{0:T(256)} %get-tuple-element.11.pair_out, s32[1]{0:T(128)} %bitcast.4.pairs, s32[64]{0:T(128)} %count.3, bf16[64,128,256]{2,1,0:T(8,128)(2,1)} %fusion.2.nk_hbm, ...), custom_call_target="tpu_custom_call" | custom-call | tf_op jit(solution)/shard_map/totals/pallas_call | solution.py:150
  131.3 23.0 %all_to_all.20 = f32[128,8,128]{2,1,0:T(8,128)S(1)} all-to-all(f32[128,8,128]{2,1,0:T(8,128)} %bitcast.13), channel_id=1, replica_groups=mesh['cam'=32,'lidar'=4] {'cam','lidar'}, dimensions={0} | all-to-all | bytes 1048576 | tf_op jit(solution)/shard_map/all_to_all | solution.py:29
  154.5 0.6 slice_divide_fusion
  155.1 15.3 %all_to_all.21 = f32[128,4,128]{2,1,0:T(4,128)} all-to-all(f32[128,4,128]{2,1,0:T(4,128)S(1)} %broadcast_in_dim.167), channel_id=1, replica_groups=mesh['cam'=32,'lidar'=4] {'cam','lidar'}, dimensions={0} | all-to-all | bytes 524288 | tf_op jit(solution)/shard_map/all_to_all | solution.py:29
  170.5 9.7 %grads.1 = bf16[64,128,256]{2,1,0:T(8,128)(2,1)} custom-call(s32[256]{0:T(256)} %get-tuple-element.6.pair_tile, s32[256]{0:T(256)} %get-tuple-element.12.pair_query, s32[1]{0:T(128)} %bitcast.4.pairs, s32[64]{0:T(128)} %count.3, bf16[64,128,256]{2,1,0:T(8,128)(2,1)} %fusion.2.nk_hbm, bf16[512,128,256]{2,1,0:T(8,128)(2,1)} %all-gather.2.cloned.1.call-done.q_hbm, ...), custom_call_target="tpu_custom_call" | custom-call | tf_op jit(solution)/shard_map/grads/pallas_call | solution.py:150
  (26 shorter events, 1.4 us)
Async XLA Ops:
  7.2 41.1 %copy-start.2 = (s32[64]{0:T(128)S(1)}, s32[64]{0:T(128)}, u32[]{:S(2)}) copy-start(s32[64]{0:T(128)} %param.9) | copy-start | bytes 772
  7.2 28.8 %copy-start.1 = (s32[4,128]{1,0:T(4,128)S(1)}, s32[4,128]{1,0:T(4,128)}, u32[]{:S(2)}) copy-start(s32[4,128]{1,0:T(4,128)} %param.13) | copy-start | bytes 6148
  7.2 117.1 %all-gather.2.cloned.1.call-start = ((), (), s32[]{:S(2)}) async-start(), calls=%async_computation.4 | async-start | bytes 33816576 | tf_op jit(solution)/shard_map/all_gather | solution.py:188
  12.3 21.1 %all-to-all-start = ((s32[128,1,1]{2,1,0:T(1,128)}), s32[128,1,1]{2,1,0:T(1,128)S(1)}, u32[]{:S(2)}, u32[]{:S(2)}) async-start(s32[128,1,1]{2,1,0:T(1,128)} %copy.28), calls=%async_computation | async-start | bytes 131072 | tf_op jit(solution)/shard_map/all_to_all | solution.py:29
  37.0 21.6 %all-to-all-start.1 = ((s32[128,4,128]{2,1,0:T(4,128)}), s32[128,4,128]{2,1,0:T(4,128)S(1)}, u32[]{:S(2)}, u32[]{:S(2)}) async-start(s32[128,4,128]{2,1,0:T(4,128)} %broadcast_select_fusion), calls=%async_computation.1 | async-start | bytes 524288 | tf_op jit(solution)/shard_map/all_to_all | solution.py:29
  58.6 65.7 %copy-start = (s32[128,4,128]{2,1,0:T(4,128)}, s32[128,4,128]{2,1,0:T(4,128)S(1)}, u32[]{:S(2)}) copy-start(s32[128,4,128]{2,1,0:T(4,128)S(1)} %all-to-all-done.1) | copy-start | bytes 786436
Sparse Core Ops, SparseCore 0:
  11.2 113.0 all-gather.1

commit v4 on v3

--- a/solution.py
+++ b/solution.py
@@ -12,7 +12,8 @@
 log2_scale = inv_temp * math.log2(math.e)
 eps = 1e-06
 TOTAL_GROUP = 8
-GRAD_GROUP = 16
+EXPO_GROUP = 8
+GRAD_GROUP = 8
 OUT_GROUP = 8
 AXES = ("cam", "lidar")
 
@@ -35,7 +36,7 @@
     )
 
 
-def over_pairs(pairs, group, sources, first, body):
+def over_pairs(pairs, group, sources, first, body, last=None):
     slots = sources[0][2].shape[0]
     ahead = slots // group - 1
     groups = (pairs + (group - 1)) // group
@@ -43,11 +44,10 @@
     def fetch(step, act):
         base = lax.rem(step, ahead + 1) * group
         for j in range(group):
+            p = step * group + j
             for hbm, index, buf, sem in sources:
-                copy = pltpu.make_async_copy(
-                    hbm.at[index[step * group + j]], buf.at[base + j], sem.at[base + j]
-                )
-                act(copy)
+                block = hbm.at[p if index is None else index[p]]
+                act(pltpu.make_async_copy(block, buf.at[base + j], sem.at[base + j]))
 
     start = lambda copy: copy.start()
     for early in range(ahead):
@@ -68,6 +68,10 @@
         base = lax.rem(step, ahead + 1) * group
         for j in range(group):
             body(step * group + j, base + j)
+        if last is not None:
+            last(step)
+
+    return groups
 
 
 def total_kernel(
@@ -92,70 +96,88 @@
     over_pairs(pairs[0], TOTAL_GROUP, sources, first, body)
 
 
+def expo_kernel(
+    pair_tile, pair_query, pairs, count, nk_hbm, q_hbm, out_hbm,
+    nk_buf, q_buf, nk_sem, q_sem, out_buf, out_sem,
+):
+    row = lax.broadcasted_iota(jnp.int32, out_buf.shape[1:], 0)
+
+    def part(step):
+        span = pl.ds(step * EXPO_GROUP, EXPO_GROUP)
+        return pltpu.make_async_copy(out_buf.at[span], out_hbm.at[span], out_sem.at[step])
+
+    def body(p, slot):
+        raw = products(nk_buf[slot], q_buf[slot])
+        live = row < count[pair_tile[p]]
+        out_buf[p] = jnp.where(live, jnp.exp2(raw * log2_scale), 0.0)
+
+    sources = [(nk_hbm, pair_tile, nk_buf, nk_sem), (q_hbm, pair_query, q_buf, q_sem)]
+    send = lambda step: part(step).start()
+    groups = over_pairs(pairs[0], EXPO_GROUP, sources, lambda: None, body, send)
+
+    @pl.loop(0, groups)
+    def _(step):
+        part(step).wait()
+
+
 def grad_kernel(
-    pair_tile, pair_query, pairs, count, nk_hbm, q_hbm, code_ref, scale_ref, out_hbm,
-    nk_buf, q_buf, nk_sem, q_sem, sum_buf, out_buf, out_sem,
+    pair_tile, pair_query, pairs, expo_hbm, q_hbm, code_ref, scale_ref, out_hbm,
+    expo_buf, q_buf, expo_sem, q_sem, sum_buf, out_buf, out_sem,
 ):
-    tiles, rows, width = sum_buf.shape
-    row = lax.broadcasted_iota(jnp.int32, (rows, code_ref.shape[1]), 0)
-    grad_row = lax.broadcasted_iota(jnp.int32, (rows, width), 0)
+    row = lax.broadcasted_iota(jnp.int32, expo_buf.shape[1:], 0)
 
     def first():
         sum_buf[...] = jnp.zeros_like(sum_buf)
 
     def body(p, slot):
         tile, query = pair_tile[p], pair_query[p]
-        raw = products(nk_buf[slot], q_buf[slot])
         code = jnp.where(p < pairs[0], code_ref[pl.ds(query, 1), :], -2)
         scale = jnp.where(code > -2, scale_ref[pl.ds(query, 1), :], 0.0)
         target = jnp.where(row == code, 1.0, 0.0)
-        weights = (jnp.exp2(raw * log2_scale) * scale - target).astype(jnp.bfloat16)
+        weights = (expo_buf[slot] * scale - target).astype(jnp.bfloat16)
         sum_buf[tile] += jnp.dot(weights, q_buf[slot], preferred_element_type=jnp.float32)
 
-    sources = [(nk_hbm, pair_tile, nk_buf, nk_sem), (q_hbm, pair_query, q_buf, q_sem)]
+    sources = [(expo_hbm, None, expo_buf, expo_sem), (q_hbm, pair_query, q_buf, q_sem)]
     over_pairs(pairs[0], GRAD_GROUP, sources, first, body)
 
     def part(group):
         span = pl.ds(group * OUT_GROUP, OUT_GROUP)
         return pltpu.make_async_copy(out_buf.at[span], out_hbm.at[span], out_sem.at[group])
 
-    @pl.loop(0, tiles // OUT_GROUP)
+    groups = out_sem.shape[0]
+
+    @pl.loop(0, groups)
     def _(group):
         for j in range(OUT_GROUP):
             tile = group * OUT_GROUP + j
-            grad = jnp.where(grad_row < count[tile], sum_buf[tile] * inv_temp, 0.0)
-            out_buf[tile] = grad.astype(jnp.bfloat16)
+            out_buf[tile] = (sum_buf[tile] * inv_temp).astype(jnp.bfloat16)
         part(group).start()
 
-    @pl.loop(0, tiles // OUT_GROUP)
+    @pl.loop(0, groups)
     def _(group):
         part(group).wait()
 
 
-def tile_call(kernel, scalars, nk, queries, tables, out_shape, slots, wide, name):
-    tiles, rows, width = nk.shape
+def tile_call(kernel, scalars, blocks, tables, out_shape, slots, wide, name):
     smem, vmem, hbm = (pl.BlockSpec(memory_space=m) for m in (pltpu.SMEM, pltpu.VMEM, pl.ANY))
-    scratch = [
-        pltpu.VMEM((slots, rows, width), jnp.bfloat16),
-        pltpu.VMEM((slots,) + queries.shape[1:], jnp.bfloat16),
-        pltpu.SemaphoreType.DMA((slots,)),
-        pltpu.SemaphoreType.DMA((slots,)),
-    ]
-    if wide:
-        scratch += [
-            pltpu.VMEM((tiles, rows, width), jnp.float32),
-            pltpu.VMEM((tiles, rows, width), jnp.bfloat16),
-            pltpu.SemaphoreType.DMA((tiles // OUT_GROUP,)),
-        ]
+    most = scalars[0].shape[0]
+    rows, width = blocks[1].shape[1:]
+    scratch = [pltpu.VMEM((slots,) + block.shape[1:], block.dtype) for block in blocks]
+    scratch += [pltpu.SemaphoreType.DMA((slots,)) for block in blocks]
     return pl.pallas_call(
         kernel,
-        in_specs=[smem] * len(scalars) + [hbm, hbm] + [vmem] * len(tables),
+        in_specs=[smem] * len(scalars) + [hbm] * len(blocks) + [vmem] * len(tables),
         out_specs=hbm if wide else vmem,
         out_shape=out_shape,
-        scratch_shapes=scratch,
+        scratch_shapes=scratch + wide,
+        cost_estimate=pl.CostEstimate(
+            flops=2 * most * rows * rows * width,
+            bytes_accessed=4 * most * rows * width,
+            transcendentals=most * rows * rows,
+        ),
         compiler_params=pltpu.CompilerParams(vmem_limit_bytes=58 * 1024 * 1024),
         name=name,
-    )(*scalars, nk, queries, *tables)
+    )(*scalars, *blocks, *tables)
 
 
 def pair_lists(code, key_dest, query_tiles):
@@ -206,28 +228,47 @@
     partial = tile_call(
         functools.partial(total_kernel, query_tiles),
         [pair_tile, pair_query, pair_out, pairs, key_count],
-        nk,
-        queries,
+        [nk, queries],
         [code],
         jax.ShapeDtypeStruct((devices * 2 * query_tiles, rows), jnp.float32),
         4 * TOTAL_GROUP,
-        False,
+        [],
         "totals",
     )
+    partial, pairs = lax.optimization_barrier((partial, pairs))
+    most = pair_tile.shape[0]
+    expo_shape = jax.ShapeDtypeStruct((most, rows, rows), jnp.float32)
+    expo = tile_call(
+        expo_kernel,
+        [pair_tile, pair_query, pairs, key_count],
+        [nk, queries],
+        [],
+        expo_shape,
+        4 * EXPO_GROUP,
+        [
+            pltpu.VMEM(expo_shape.shape, jnp.float32),
+            pltpu.SemaphoreType.DMA((most // EXPO_GROUP,)),
+        ],
+        "expos",
+    )
     partial = partial.reshape(devices, 2 * query_tiles, rows)
-    arrived = jnp.sum(exchange(partial), axis=0)
+    arrived, expo = lax.optimization_barrier((exchange(partial), expo))
+    arrived = jnp.sum(arrived, axis=0)
     total, picked = arrived[:query_tiles], arrived[query_tiles:]
     scale = exchange(jnp.broadcast_to((1.0 / total)[None], (devices, query_tiles, rows)))
     loss = jnp.log(total) - picked
     key_grad = tile_call(
         grad_kernel,
-        [pair_tile, pair_query, pairs, key_count],
-        nk,
-        queries,
+        [pair_tile, pair_query, pairs],
+        [expo, queries],
         [code, scale.reshape(devices * query_tiles, rows)],
         jax.ShapeDtypeStruct((tiles, rows, width), jnp.bfloat16),
-        3 * GRAD_GROUP,
-        True,
+        5 * GRAD_GROUP,
+        [
+            pltpu.VMEM((tiles, rows, width), jnp.float32),
+            pltpu.VMEM((tiles, rows, width), jnp.bfloat16),
+            pltpu.SemaphoreType.DMA((tiles // OUT_GROUP,)),
+        ],
         "grads",
     )
     return (loss, key_grad)

time: 190 us -> 191 us (level); the launches traced: 187 us -> 192 us
  blocking collectives: 38.4 us -> 18.7 us
  Pallas kernels: 16.8 us -> 27 us
  starting transfers between devices: 21 us -> 30.4 us
  waiting for transfers between devices: 73.1 us -> 77.8 us
    all_to_all x2 -> x1, blocking collectives: 38.4 us -> 18.7 us  [exchange(): return lax.all_to_all(x, AXES, split_axis=0, concat_axis=0, tiled=True)]
    pallas_call x2 -> x3, Pallas kernels: 16.8 us -> 27 us  [tile_call(): pl.pallas_call(kernel, in_specs=[smem] * len(scalars) + [hbm] * len(block...]
    all_to_all x2 -> x3, starting transfers between devices: 20.9 us -> 30.4 us  [exchange(): return lax.all_to_all(x, AXES, split_axis=0, concat_axis=0, tiled=True)]
    all_to_all x2 -> x3, waiting for transfers between devices: 10.5 us -> 15.1 us  [exchange(): return lax.all_to_all(x, AXES, split_axis=0, concat_axis=0, tiled=True)]
  transfers between devices with their start and end apart: 3 -> 4, of which waited for: 3 -> 4; matrix products, arithmetic and copies ran while one was open for 10% -> 10% of each run, Pallas kernels for 0% -> 5%
where the time goes in v4:
time: 191 us; the launch traced here: 192 us
  waiting for transfers between devices  77.8 us (41%)
  starting transfers between devices  30.4 us (16%)
  Pallas kernels  27 us (14%)
  other arithmetic  20 us (10%)
  blocking collectives  18.7 us (10%)
  between operations  15.5 us (8%)
  local copies, waits for them, and re-layouts  2.43 us (1%)
    all_gather x1, waiting for transfers between devices, shards(): queries = lax.all_gather(unit_rows(query_feats), AXES, axis=0, tiled=True)  62.6 us
    all_to_all x3, starting transfers between devices, exchange(): return lax.all_to_all(x, AXES, split_axis=0, concat_axis=0, tiled=True)  30.4 us
    pallas_call x3, Pallas kernels, tile_call(): pl.pallas_call(kernel, in_specs=[smem] * len(scalars) + [hbm] * len(block...  27 us
    all_to_all x1, blocking collectives, exchange(): return lax.all_to_all(x, AXES, split_axis=0, concat_axis=0, tiled=True)  18.7 us
    all_to_all x3, waiting for transfers between devices, exchange(): return lax.all_to_all(x, AXES, split_axis=0, concat_axis=0, tiled=True)  15.1 us
    convert_element_type x2, other arithmetic, unit_rows(): return scaled.astype(jnp.bfloat16)  6.02 us
    reduce_sum x2, other arithmetic, unit_rows(): jnp.mean(xf * xf, axis=-1, keepdims=True) + eps  4.52 us
  transfers between devices with their start and end apart: 4, of which 4 were waited for; matrix products, arithmetic and copies ran while one was open for 10% of the time, Pallas kernels for 5%

profile of v4, /device:TPU:1, one launch (start us, length us, event | category | flops | bytes accessed | tf_op | source)
XLA Modules:
  0.0 191.8 jit_solution(5660493319034761289)
XLA Ops:
  7.2 1.1 fusion.3
  8.3 1.8 fusion.5
  10.2 0.7 broadcast_add_fusion
  10.8 0.7 select_reduce_fusion.7
  11.6 0.7 copy.28
  12.3 11.5 %all-to-all-start = ((s32[128,1,1]{2,1,0:T(1,128)}), s32[128,1,1]{2,1,0:T(1,128)S(1)}, u32[]{:S(2)}, u32[]{:S(2)}) async-start(s32[128,1,1]{2,1,0:T(1,128)} %copy.28), calls=%async_computation | async-start | bytes 131072 | tf_op jit(solution)/shard_map/all_to_all | solution.py:30
  23.8 0.7 broadcast_in_dim.162
  24.7 0.7 and_select_fusion.2
  25.3 3.4 %fusion = f32[64,128]{1,0:T(8,128)S(1)} fusion(bf16[64,128,256]{2,1,0:T(8,128)(2,1)} %param.7), kind=kLoop, calls=%fused_computation.2 | loop fusion | flops 6283264 | bytes 4227072 | tf_op jit(solution)/shard_map/reduce_sum | solution.py:24
  28.8 4.2 %fusion.2.nk_hbm = bf16[64,128,256]{2,1,0:T(8,128)(2,1)} fusion(bf16[64,128,256]{2,1,0:T(8,128)(2,1)} %param.7, f32[64,128]{1,0:T(8,128)S(1)} %add_rsqrt_fusion), kind=kLoop, calls=%fused_computation.4 | loop fusion | flops 8388608 | bytes 8421376 | tf_op jit(solution)/shard_map/convert_element_type | solution.py:26
  33.5 2.3 %reduce.2 = s32[128]{0:T(128)S(1)} reduce(s32[128,1,1]{2,1,0:T(1,128)S(1)} %all-to-all-done, s32[]{:T(128)} %constant.62.clone.1), dimensions={1,2}, to_apply=%all_to_all.12.reduce_sub_computation | reduce | bytes 1028 | tf_op jit(solution)/shard_map/all_to_all | solution.py:30
  36.0 1.0 broadcast_select_fusion
  37.1 9.3 %all-to-all-start.1 = ((s32[128,4,128]{2,1,0:T(4,128)}), s32[128,4,128]{2,1,0:T(4,128)S(1)}, u32[]{:S(2)}, u32[]{:S(2)}) async-start(s32[128,4,128]{2,1,0:T(4,128)} %broadcast_select_fusion), calls=%async_computation.1 | async-start | bytes 524288 | tf_op jit(solution)/shard_map/all_to_all | solution.py:30
  48.3 10.2 %all-to-all-done.1 = s32[128,4,128]{2,1,0:T(4,128)S(1)} async-done(((s32[128,4,128]{2,1,0:T(4,128)}), s32[128,4,128]{2,1,0:T(4,128)S(1)}, u32[]{:S(2)}, u32[]{:S(2)}) %all-to-all-start.1) | async-done | bytes 262176 | tf_op jit(solution)/shard_map/all_to_all | solution.py:30
  58.6 0.8 select_reduce_fusion.4
  59.7 0.8 select_reduce_fusion
  60.5 1.3 fusion.9
  61.7 62.6 %all-gather.2.cloned.1.call-done.q_hbm = bf16[512,128,256]{2,1,0:T(8,128)(2,1)} async-done(((bf16[4,128,256]{2,1,0:T(8,128)(2,1)}), bf16[512,128,256]{2,1,0:T(8,128)(2,1)}) %all-gather.2.cloned.1.call-update) | async-done | bytes 33554448 | tf_op jit(solution)/shard_map/all_gather | solution.py:210
  124.3 8.8 %totals.1 = f32[1024,128]{1,0:T(8,128)} custom-call(s32[256]{0:T(256)} %get-tuple-element.14.pair_tile, s32[256]{0:T(256)} %get-tuple-element.20.pair_query, s32[256]{0:T(256)} %get-tuple-element.19.pair_out, s32[1]{0:T(128)} %bitcast.4.pairs, s32[64]{0:T(128)} %count.3, bf16[64,128,256]{2,1,0:T(8,128)(2,1)} %fusion.2.nk_hbm, ...), custom_call_target="tpu_custom_call" | custom-call | flops 2147483648 | bytes 33554432 | tf_op jit(solution)/shard_map/totals/pallas_call | solution.py:167
  133.1 9.6 %all-to-all-start.2 = ((f32[128,8,128]{2,1,0:T(8,128)}), f32[128,8,128]{2,1,0:T(8,128)S(1)}, u32[]{:S(2)}, u32[]{:S(2)}) async-start(f32[128,8,128]{2,1,0:T(8,128)} %bitcast.13), calls=%async_computation.2 | async-start | bytes 1048576 | tf_op jit(solution)/shard_map/all_to_all | solution.py:30
  142.7 9.2 %expos.1.expo_hbm = f32[256,128,128]{2,1,0:T(8,128)} custom-call(s32[256]{0:T(256)} %get-tuple-element.14.pair_tile, s32[256]{0:T(256)} %get-tuple-element.20.pair_query, s32[1]{0:T(128)} %bitcast.4.pairs, s32[64]{0:T(128)} %count.3, bf16[64,128,256]{2,1,0:T(8,128)(2,1)} %fusion.2.nk_hbm, bf16[512,128,256]{2,1,0:T(8,128)(2,1)} %all-gather.2.cloned.1.call-done.q_hbm), custom_call_target="tpu_custom_call" | custom-call | flops 2147483648 | bytes 33554432 | tf_op jit(solution)/shard_map/expos/pallas_call | solution.py:167
  152.0 4.5 %all-to-all-done.2 = f32[128,8,128]{2,1,0:T(8,128)S(1)} async-done(((f32[128,8,128]{2,1,0:T(8,128)}), f32[128,8,128]{2,1,0:T(8,128)S(1)}, u32[]{:S(2)}, u32[]{:S(2)}) %all-to-all-start.2) | async-done | bytes 524320 | tf_op jit(solution)/shard_map/all_to_all | solution.py:30
  157.3 18.7 %all_to_all.20 = f32[128,4,128]{2,1,0:T(4,128)} all-to-all(f32[128,4,128]{2,1,0:T(4,128)S(1)} %broadcast_in_dim.167), channel_id=1, replica_groups=mesh['cam'=32,'lidar'=4] {'cam','lidar'}, dimensions={0} | all-to-all | bytes 524288 | tf_op jit(solution)/shard_map/all_to_all | solution.py:30
  175.9 9.0 %grads.1 = bf16[64,128,256]{2,1,0:T(8,128)(2,1)} custom-call(s32[256]{0:T(256)} %get-tuple-element.14.pair_tile, s32[256]{0:T(256)} %get-tuple-element.20.pair_query, s32[1]{0:T(128)} %bitcast.4.pairs, f32[256,128,128]{2,1,0:T(8,128)} %expos.1.expo_hbm, bf16[512,128,256]{2,1,0:T(8,128)(2,1)} %all-gather.2.cloned.1.call-done.q_hbm, s32[512,128]{1,0:T(8,128)} %bitcast.12, ...), custom_call_target="tpu_custom_call" | custom-call | flops 2147483648 | bytes 33554432 | tf_op jit(solution)/shard_map/grads/pallas_call | solution.py:167
  (28 shorter events, 2.6 us)
Async XLA Ops:
  7.2 41.0 %copy-start.2 = (s32[64]{0:T(128)S(1)}, s32[64]{0:T(128)}, u32[]{:S(2)}) copy-start(s32[64]{0:T(128)} %param.9) | copy-start | bytes 772
  7.2 28.8 %copy-start.1 = (s32[4,128]{1,0:T(4,128)S(1)}, s32[4,128]{1,0:T(4,128)}, u32[]{:S(2)}) copy-start(s32[4,128]{1,0:T(4,128)} %param.13) | copy-start | bytes 6148
  7.2 117.2 %all-gather.2.cloned.1.call-start = ((), (), s32[]{:S(2)}) async-start(), calls=%async_computation.4 | async-start | bytes 33816576 | tf_op jit(solution)/shard_map/all_gather | solution.py:210
  12.3 21.1 %all-to-all-start = ((s32[128,1,1]{2,1,0:T(1,128)}), s32[128,1,1]{2,1,0:T(1,128)S(1)}, u32[]{:S(2)}, u32[]{:S(2)}) async-start(s32[128,1,1]{2,1,0:T(1,128)} %copy.28), calls=%async_computation | async-start | bytes 131072 | tf_op jit(solution)/shard_map/all_to_all | solution.py:30
  37.1 21.4 %all-to-all-start.1 = ((s32[128,4,128]{2,1,0:T(4,128)}), s32[128,4,128]{2,1,0:T(4,128)S(1)}, u32[]{:S(2)}, u32[]{:S(2)}) async-start(s32[128,4,128]{2,1,0:T(4,128)} %broadcast_select_fusion), calls=%async_computation.1 | async-start | bytes 524288 | tf_op jit(solution)/shard_map/all_to_all | solution.py:30
  58.5 65.9 %copy-start = (s32[128,4,128]{2,1,0:T(4,128)}, s32[128,4,128]{2,1,0:T(4,128)S(1)}, u32[]{:S(2)}) copy-start(s32[128,4,128]{2,1,0:T(4,128)S(1)} %all-to-all-done.1) | copy-start | bytes 786436
  133.1 23.4 %all-to-all-start.2 = ((f32[128,8,128]{2,1,0:T(8,128)}), f32[128,8,128]{2,1,0:T(8,128)S(1)}, u32[]{:S(2)}, u32[]{:S(2)}) async-start(f32[128,8,128]{2,1,0:T(8,128)} %bitcast.13), calls=%async_computation.2 | async-start | bytes 1048576 | tf_op jit(solution)/shard_map/all_to_all | solution.py:30
Sparse Core Ops, SparseCore 0:
  11.2 113.1 all-gather.1

commit v5 on v4

--- a/solution.py
+++ b/solution.py
@@ -12,7 +12,6 @@
 log2_scale = inv_temp * math.log2(math.e)
 eps = 1e-06
 TOTAL_GROUP = 8
-EXPO_GROUP = 8
 GRAD_GROUP = 8
 OUT_GROUP = 8
 AXES = ("cam", "lidar")
@@ -75,9 +74,13 @@
 
 
 def total_kernel(
-    slots, pair_tile, pair_query, pair_out, pairs, count, nk_hbm, q_hbm, code_ref, out_ref,
-    nk_buf, q_buf, nk_sem, q_sem,
+    slots, pair_tile, pair_query, pair_out, pairs, count, nk_hbm, q_hbm, code_ref,
+    out_ref, expo_hbm, nk_buf, q_buf, nk_sem, q_sem, expo_buf, expo_sem,
 ):
+    def part(step):
+        span = pl.ds(step * TOTAL_GROUP, TOTAL_GROUP)
+        return pltpu.make_async_copy(expo_buf.at[span], expo_hbm.at[span], expo_sem.at[step])
+
     row = lax.broadcasted_iota(jnp.int32, (nk_buf.shape[1], code_ref.shape[1]), 0)
 
     def first():
@@ -87,33 +90,15 @@
         raw = products(nk_buf[slot], q_buf[slot])
         code = code_ref[pl.ds(pair_query[p], 1), :]
         expo = jnp.where(row < count[pair_tile[p]], jnp.exp2(raw * log2_scale), 0.0)
+        expo_buf[p] = expo
         total = jnp.sum(expo, axis=0, keepdims=True)
         picked = jnp.sum(jnp.where(row == code, raw, 0.0), axis=0, keepdims=True)
         out_ref[pl.ds(pair_out[p], 1), :] = jnp.where(code > -2, total, 0.0)
         out_ref[pl.ds(pair_out[p] + slots, 1), :] = picked * inv_temp
 
     sources = [(nk_hbm, pair_tile, nk_buf, nk_sem), (q_hbm, pair_query, q_buf, q_sem)]
-    over_pairs(pairs[0], TOTAL_GROUP, sources, first, body)
-
-
-def expo_kernel(
-    pair_tile, pair_query, pairs, count, nk_hbm, q_hbm, out_hbm,
-    nk_buf, q_buf, nk_sem, q_sem, out_buf, out_sem,
-):
-    row = lax.broadcasted_iota(jnp.int32, out_buf.shape[1:], 0)
-
-    def part(step):
-        span = pl.ds(step * EXPO_GROUP, EXPO_GROUP)
-        return pltpu.make_async_copy(out_buf.at[span], out_hbm.at[span], out_sem.at[step])
-
-    def body(p, slot):
-        raw = products(nk_buf[slot], q_buf[slot])
-        live = row < count[pair_tile[p]]
-        out_buf[p] = jnp.where(live, jnp.exp2(raw * log2_scale), 0.0)
-
-    sources = [(nk_hbm, pair_tile, nk_buf, nk_sem), (q_hbm, pair_query, q_buf, q_sem)]
     send = lambda step: part(step).start()
-    groups = over_pairs(pairs[0], EXPO_GROUP, sources, lambda: None, body, send)
+    groups = over_pairs(pairs[0], TOTAL_GROUP, sources, first, body, send)
 
     @pl.loop(0, groups)
     def _(step):
@@ -122,43 +107,57 @@
 
 def grad_kernel(
     pair_tile, pair_query, pairs, expo_hbm, q_hbm, code_ref, scale_ref, out_hbm,
-    expo_buf, q_buf, expo_sem, q_sem, sum_buf, out_buf, out_sem,
+    expo_buf, q_buf, expo_sem, q_sem, sum_buf, out_buf, out_sem, sent,
 ):
     row = lax.broadcasted_iota(jnp.int32, expo_buf.shape[1:], 0)
+    most = pair_tile.shape[0]
+    tiles = out_hbm.shape[0]
+
+    def part(group):
+        span = pl.ds(group * OUT_GROUP, OUT_GROUP)
+        return pltpu.make_async_copy(out_buf.at[span], out_hbm.at[span], out_sem.at[group])
+
+    def send_until(tile):
+        ready = jnp.maximum(tile // OUT_GROUP, sent[0])
+
+        @pl.loop(sent[0], ready)
+        def _(group):
+            part(group).start()
+
+        sent[0] = ready
 
     def first():
+        out_buf[...] = jnp.zeros_like(out_buf)
         sum_buf[...] = jnp.zeros_like(sum_buf)
+        sent[0] = 0
 
     def body(p, slot):
+        valid = p < pairs[0]
         tile, query = pair_tile[p], pair_query[p]
-        code = jnp.where(p < pairs[0], code_ref[pl.ds(query, 1), :], -2)
+        code = code_ref[pl.ds(query, 1), :]
         scale = jnp.where(code > -2, scale_ref[pl.ds(query, 1), :], 0.0)
         target = jnp.where(row == code, 1.0, 0.0)
         weights = (expo_buf[slot] * scale - target).astype(jnp.bfloat16)
-        sum_buf[tile] += jnp.dot(weights, q_buf[slot], preferred_element_type=jnp.float32)
+        grad = jnp.dot(weights, q_buf[slot], preferred_element_type=jnp.float32)
+        same = pair_tile[jnp.maximum(p - 1, 0)] == tile
+        grad = jnp.where(same, sum_buf[...], 0.0) + grad
+        sum_buf[...] = grad
+        out_buf[jnp.where(valid, tile, tiles)] = (grad * inv_temp).astype(jnp.bfloat16)
+
+    def last(step):
+        ahead = (step + 1) * GRAD_GROUP
+        send_until(jnp.where(ahead < pairs[0], pair_tile[jnp.minimum(ahead, most - 1)], 0))
 
     sources = [(expo_hbm, None, expo_buf, expo_sem), (q_hbm, pair_query, q_buf, q_sem)]
-    over_pairs(pairs[0], GRAD_GROUP, sources, first, body)
-
-    def part(group):
-        span = pl.ds(group * OUT_GROUP, OUT_GROUP)
-        return pltpu.make_async_copy(out_buf.at[span], out_hbm.at[span], out_sem.at[group])
-
-    groups = out_sem.shape[0]
-
-    @pl.loop(0, groups)
-    def _(group):
-        for j in range(OUT_GROUP):
-            tile = group * OUT_GROUP + j
-            out_buf[tile] = (sum_buf[tile] * inv_temp).astype(jnp.bfloat16)
-        part(group).start()
-
-    @pl.loop(0, groups)
+    over_pairs(pairs[0], GRAD_GROUP, sources, first, body, last)
+    send_until(tiles)
+
+    @pl.loop(0, tiles // OUT_GROUP)
     def _(group):
         part(group).wait()
 
 
-def tile_call(kernel, scalars, blocks, tables, out_shape, slots, wide, name):
+def tile_call(kernel, scalars, blocks, tables, out_shape, out_spaces, slots, wide, name):
     smem, vmem, hbm = (pl.BlockSpec(memory_space=m) for m in (pltpu.SMEM, pltpu.VMEM, pl.ANY))
     most = scalars[0].shape[0]
     rows, width = blocks[1].shape[1:]
@@ -167,7 +166,7 @@
     return pl.pallas_call(
         kernel,
         in_specs=[smem] * len(scalars) + [hbm] * len(blocks) + [vmem] * len(tables),
-        out_specs=hbm if wide else vmem,
+        out_specs=[pl.BlockSpec(memory_space=m) for m in out_spaces],
         out_shape=out_shape,
         scratch_shapes=scratch + wide,
         cost_estimate=pl.CostEstimate(
@@ -225,49 +224,40 @@
     nk = unit_rows(key_feats)
     pair_tile, pair_query, pair_out, pairs = pair_lists(code, key_dest, query_tiles)
     code = code.reshape(devices * query_tiles, rows)
-    partial = tile_call(
+    most = pair_tile.shape[0]
+    expo_shape = jax.ShapeDtypeStruct((most, rows, rows), jnp.float32)
+    partial, expo = tile_call(
         functools.partial(total_kernel, query_tiles),
         [pair_tile, pair_query, pair_out, pairs, key_count],
         [nk, queries],
         [code],
-        jax.ShapeDtypeStruct((devices * 2 * query_tiles, rows), jnp.float32),
+        [jax.ShapeDtypeStruct((devices * 2 * query_tiles, rows), jnp.float32), expo_shape],
+        [pltpu.VMEM, pl.ANY],
         4 * TOTAL_GROUP,
-        [],
-        "totals",
-    )
-    partial, pairs = lax.optimization_barrier((partial, pairs))
-    most = pair_tile.shape[0]
-    expo_shape = jax.ShapeDtypeStruct((most, rows, rows), jnp.float32)
-    expo = tile_call(
-        expo_kernel,
-        [pair_tile, pair_query, pairs, key_count],
-        [nk, queries],
-        [],
-        expo_shape,
-        4 * EXPO_GROUP,
         [
             pltpu.VMEM(expo_shape.shape, jnp.float32),
-            pltpu.SemaphoreType.DMA((most // EXPO_GROUP,)),
+            pltpu.SemaphoreType.DMA((most // TOTAL_GROUP,)),
         ],
-        "expos",
+        "totals",
     )
     partial = partial.reshape(devices, 2 * query_tiles, rows)
-    arrived, expo = lax.optimization_barrier((exchange(partial), expo))
-    arrived = jnp.sum(arrived, axis=0)
+    arrived = jnp.sum(exchange(partial), axis=0)
     total, picked = arrived[:query_tiles], arrived[query_tiles:]
     scale = exchange(jnp.broadcast_to((1.0 / total)[None], (devices, query_tiles, rows)))
     loss = jnp.log(total) - picked
-    key_grad = tile_call(
+    (key_grad,) = tile_call(
         grad_kernel,
         [pair_tile, pair_query, pairs],
         [expo, queries],
         [code, scale.reshape(devices * query_tiles, rows)],
-        jax.ShapeDtypeStruct((tiles, rows, width), jnp.bfloat16),
+        [jax.ShapeDtypeStruct((tiles, rows, width), jnp.bfloat16)],
+        [pl.ANY],
         5 * GRAD_GROUP,
         [
-            pltpu.VMEM((tiles, rows, width), jnp.float32),
-            pltpu.VMEM((tiles, rows, width), jnp.bfloat16),
+            pltpu.VMEM((rows, width), jnp.float32),
+            pltpu.VMEM((tiles + 1, rows, width), jnp.bfloat16),
             pltpu.SemaphoreType.DMA((tiles // OUT_GROUP,)),
+            pltpu.SMEM((1,), jnp.int32),
         ],
         "grads",
     )

time: 191 us -> 190 us (level); the launches traced: 192 us -> 189 us
  blocking collectives: 18.7 us -> 36.9 us
  starting transfers between devices: 30.4 us -> 20.8 us
  Pallas kernels: 27 us -> 19.7 us
  waiting for transfers between devices: 77.8 us -> 73.2 us
    all_to_all x1 -> x2, blocking collectives: 18.7 us -> 36.9 us  [exchange(): return lax.all_to_all(x, AXES, split_axis=0, concat_axis=0, tiled=True)]
    all_to_all x3 -> x2, starting transfers between devices: 30.4 us -> 20.8 us  [exchange(): return lax.all_to_all(x, AXES, split_axis=0, concat_axis=0, tiled=True)]
    pallas_call x3 -> x2, Pallas kernels: 27 us -> 19.7 us  [tile_call(): pl.pallas_call(kernel, in_specs=[smem] * len(scalars) + [hbm] * len(block...]
    all_to_all x3 -> x2, waiting for transfers between devices: 15.1 us -> 10.6 us  [exchange(): return lax.all_to_all(x, AXES, split_axis=0, concat_axis=0, tiled=True)]
  transfers between devices with their start and end apart: 4 -> 3, of which waited for: 4 -> 3; matrix products, arithmetic and copies ran while one was open for 10% -> 10% of each run, Pallas kernels for 5% -> 0%
where the time goes in v5:
time: 190 us; the launch traced here: 189 us
  waiting for transfers between devices  73.2 us (39%)
  blocking collectives  36.9 us (19%)
  starting transfers between devices  20.8 us (11%)
  other arithmetic  20 us (11%)
  Pallas kernels  19.7 us (10%)
  between operations  15.5 us (8%)
  local copies, waits for them, and re-layouts  2.43 us (1%)
    all_gather x1, waiting for transfers between devices, shards(): queries = lax.all_gather(unit_rows(query_feats), AXES, axis=0, tiled=True)  62.6 us
    all_to_all x2, blocking collectives, exchange(): return lax.all_to_all(x, AXES, split_axis=0, concat_axis=0, tiled=True)  36.9 us
    all_to_all x2, starting transfers between devices, exchange(): return lax.all_to_all(x, AXES, split_axis=0, concat_axis=0, tiled=True)  20.8 us
    pallas_call x2, Pallas kernels, tile_call(): pl.pallas_call(kernel, in_specs=[smem] * len(scalars) + [hbm] * len(block...  19.7 us
    all_to_all x2, waiting for transfers between devices, exchange(): return lax.all_to_all(x, AXES, split_axis=0, concat_axis=0, tiled=True)  10.6 us
    convert_element_type x2, other arithmetic, unit_rows(): return scaled.astype(jnp.bfloat16)  6.02 us
    reduce_sum x2, other arithmetic, unit_rows(): jnp.mean(xf * xf, axis=-1, keepdims=True) + eps  4.52 us
  transfers between devices with their start and end apart: 3, of which 3 were waited for; matrix products, arithmetic and copies ran while one was open for 10% of the time, Pallas kernels for 0%

profile of v5, /device:TPU:1, one launch (start us, length us, event | category | flops | bytes accessed | tf_op | source)
XLA Modules:
  0.0 188.6 jit_solution(1449990569619934375)
XLA Ops:
  7.2 1.1 fusion.3
  8.3 1.8 fusion.5
  10.2 0.7 broadcast_add_fusion
  10.8 0.7 select_reduce_fusion.7
  11.6 0.7 copy.28
  12.3 11.5 %all-to-all-start = ((s32[128,1,1]{2,1,0:T(1,128)}), s32[128,1,1]{2,1,0:T(1,128)S(1)}, u32[]{:S(2)}, u32[]{:S(2)}) async-start(s32[128,1,1]{2,1,0:T(1,128)} %copy.28), calls=%async_computation | async-start | bytes 131072 | tf_op jit(solution)/shard_map/all_to_all | solution.py:29
  23.8 0.7 broadcast_in_dim.162
  24.7 0.7 and_select_fusion.2
  25.3 3.4 %fusion = f32[64,128]{1,0:T(8,128)S(1)} fusion(bf16[64,128,256]{2,1,0:T(8,128)(2,1)} %param.7), kind=kLoop, calls=%fused_computation.2 | loop fusion | flops 6283264 | bytes 4227072 | tf_op jit(solution)/shard_map/reduce_sum | solution.py:23
  28.8 4.2 %fusion.2.nk_hbm = bf16[64,128,256]{2,1,0:T(8,128)(2,1)} fusion(bf16[64,128,256]{2,1,0:T(8,128)(2,1)} %param.7, f32[64,128]{1,0:T(8,128)S(1)} %add_rsqrt_fusion), kind=kLoop, calls=%fused_computation.4 | loop fusion | flops 8388608 | bytes 8421376 | tf_op jit(solution)/shard_map/convert_element_type | solution.py:25
  33.5 2.3 %reduce.2 = s32[128]{0:T(128)S(1)} reduce(s32[128,1,1]{2,1,0:T(1,128)S(1)} %all-to-all-done, s32[]{:T(128)} %constant.62.clone.1), dimensions={1,2}, to_apply=%all_to_all.12.reduce_sub_computation | reduce | bytes 1028 | tf_op jit(solution)/shard_map/all_to_all | solution.py:29
  36.0 1.0 broadcast_select_fusion
  37.1 9.3 %all-to-all-start.1 = ((s32[128,4,128]{2,1,0:T(4,128)}), s32[128,4,128]{2,1,0:T(4,128)S(1)}, u32[]{:S(2)}, u32[]{:S(2)}) async-start(s32[128,4,128]{2,1,0:T(4,128)} %broadcast_select_fusion), calls=%async_computation.1 | async-start | bytes 524288 | tf_op jit(solution)/shard_map/all_to_all | solution.py:29
  46.4 0.5 slice.14
  48.3 10.2 %all-to-all-done.1 = s32[128,4,128]{2,1,0:T(4,128)S(1)} async-done(((s32[128,4,128]{2,1,0:T(4,128)}), s32[128,4,128]{2,1,0:T(4,128)S(1)}, u32[]{:S(2)}, u32[]{:S(2)}) %all-to-all-start.1) | async-done | bytes 262176 | tf_op jit(solution)/shard_map/all_to_all | solution.py:29
  58.6 0.8 select_reduce_fusion.4
  59.7 0.8 select_reduce_fusion
  60.5 1.3 fusion.9
  61.7 62.6 %all-gather.2.cloned.1.call-done.q_hbm = bf16[512,128,256]{2,1,0:T(8,128)(2,1)} async-done(((bf16[4,128,256]{2,1,0:T(8,128)(2,1)}), bf16[512,128,256]{2,1,0:T(8,128)(2,1)}) %all-gather.2.cloned.1.call-update) | async-done | bytes 33554448 | tf_op jit(solution)/shard_map/all_gather | solution.py:209
  124.3 11.1 %totals.1 = (f32[1024,128]{1,0:T(8,128)}, f32[256,128,128]{2,1,0:T(8,128)}) custom-call(s32[256]{0:T(256)} %get-tuple-element.10.pair_tile, s32[256]{0:T(256)} %get-tuple-element.16.pair_query, s32[256]{0:T(256)} %get-tuple-element.15.pair_out, s32[1]{0:T(128)} %bitcast.4.pairs, s32[64]{0:T(128)} %count.1, bf16[64,128,256]{2,1,0:T(8,128)(2,1)} %fusion.2.nk_hbm, ...), custom_call_target="tpu_custom_call" | custom-call | flops 2147483648 | bytes 33554432 | tf_op jit(solution)/shard_map/totals/pallas_call | solution.py:166
  135.4 21.6 %all_to_all.20 = f32[128,8,128]{2,1,0:T(8,128)S(1)} all-to-all(f32[128,8,128]{2,1,0:T(8,128)} %bitcast.14), channel_id=1, replica_groups=mesh['cam'=32,'lidar'=4] {'cam','lidar'}, dimensions={0} | all-to-all | bytes 1048576 | tf_op jit(solution)/shard_map/all_to_all | solution.py:29
  157.2 0.6 slice_divide_fusion
  157.8 15.3 %all_to_all.21 = f32[128,4,128]{2,1,0:T(4,128)} all-to-all(f32[128,4,128]{2,1,0:T(4,128)S(1)} %broadcast_in_dim.167), channel_id=1, replica_groups=mesh['cam'=32,'lidar'=4] {'cam','lidar'}, dimensions={0} | all-to-all | bytes 524288 | tf_op jit(solution)/shard_map/all_to_all | solution.py:29
  173.1 8.6 %grads.1 = bf16[64,128,256]{2,1,0:T(8,128)(2,1)} custom-call(s32[256]{0:T(256)} %get-tuple-element.10.pair_tile, s32[256]{0:T(256)} %get-tuple-element.16.pair_query, s32[1]{0:T(128)} %bitcast.4.pairs, f32[256,128,128]{2,1,0:T(8,128)} %get-tuple-element.5.expo_hbm, bf16[512,128,256]{2,1,0:T(8,128)(2,1)} %all-gather.2.cloned.1.call-done.q_hbm, ...), custom_call_target="tpu_custom_call" | custom-call | flops 2147483648 | bytes 33554432 | tf_op jit(solution)/shard_map/grads/pallas_call | solution.py:166
  (26 shorter events, 1.5 us)
Async XLA Ops:
  7.2 41.0 %copy-start.2 = (s32[64]{0:T(128)S(1)}, s32[64]{0:T(128)}, u32[]{:S(2)}) copy-start(s32[64]{0:T(128)} %param.9) | copy-start | bytes 772
  7.2 28.8 %copy-start.1 = (s32[4,128]{1,0:T(4,128)S(1)}, s32[4,128]{1,0:T(4,128)}, u32[]{:S(2)}) copy-start(s32[4,128]{1,0:T(4,128)} %param.13) | copy-start | bytes 6148
  7.2 117.2 %all-gather.2.cloned.1.call-start = ((), (), s32[]{:S(2)}) async-start(), calls=%async_computation.4 | async-start | bytes 33816576 | tf_op jit(solution)/shard_map/all_gather | solution.py:209
  12.3 21.1 %all-to-all-start = ((s32[128,1,1]{2,1,0:T(1,128)}), s32[128,1,1]{2,1,0:T(1,128)S(1)}, u32[]{:S(2)}, u32[]{:S(2)}) async-start(s32[128,1,1]{2,1,0:T(1,128)} %copy.28), calls=%async_computation | async-start | bytes 131072 | tf_op jit(solution)/shard_map/all_to_all | solution.py:29
  37.1 21.4 %all-to-all-start.1 = ((s32[128,4,128]{2,1,0:T(4,128)}), s32[128,4,128]{2,1,0:T(4,128)S(1)}, u32[]{:S(2)}, u32[]{:S(2)}) async-start(s32[128,4,128]{2,1,0:T(4,128)} %broadcast_select_fusion), calls=%async_computation.1 | async-start | bytes 524288 | tf_op jit(solution)/shard_map/all_to_all | solution.py:29
  58.5 65.9 %copy-start = (s32[128,4,128]{2,1,0:T(4,128)}, s32[128,4,128]{2,1,0:T(4,128)S(1)}, u32[]{:S(2)}) copy-start(s32[128,4,128]{2,1,0:T(4,128)S(1)} %all-to-all-done.1) | copy-start | bytes 786436
Sparse Core Ops, SparseCore 0:
  11.2 113.1 all-gather.1

commit v6 on v5

--- a/solution.py
+++ b/solution.py
@@ -12,8 +12,12 @@
 log2_scale = inv_temp * math.log2(math.e)
 eps = 1e-06
 TOTAL_GROUP = 8
+TOTAL_AHEAD = 3
 GRAD_GROUP = 8
 OUT_GROUP = 8
+TOTAL_MIB = 5
+GRAD_MIB = 5
+SHARE_MIB = 2
 AXES = ("cam", "lidar")
 
 
@@ -35,18 +39,16 @@
     )
 
 
-def over_pairs(pairs, group, sources, first, body, last=None):
-    slots = sources[0][2].shape[0]
-    ahead = slots // group - 1
+def over_pairs(pairs, group, ahead, sources, first, body, last=None):
     groups = (pairs + (group - 1)) // group
 
     def fetch(step, act):
         base = lax.rem(step, ahead + 1) * group
         for j in range(group):
             p = step * group + j
-            for hbm, index, buf, sem in sources:
-                block = hbm.at[p if index is None else index[p]]
-                act(pltpu.make_async_copy(block, buf.at[base + j], sem.at[base + j]))
+            for hbm, index, buf, sem, ring in sources:
+                place = buf.at[base + j if ring else p]
+                act(pltpu.make_async_copy(hbm.at[index[p]], place, sem.at[base + j]))
 
     start = lambda copy: copy.start()
     for early in range(ahead):
@@ -70,46 +72,46 @@
         if last is not None:
             last(step)
 
-    return groups
-
 
 def total_kernel(
-    slots, pair_tile, pair_query, pair_out, pairs, count, nk_hbm, q_hbm, code_ref,
-    out_ref, expo_hbm, nk_buf, q_buf, nk_sem, q_sem, expo_buf, expo_sem,
+    half, pair_tile, pair_query, pair_out, pairs, count, nk_hbm, q_hbm, code_ref,
+    out_ref, expo_ref, q_ref, nk_buf, nk_sem, q_sem,
 ):
-    def part(step):
-        span = pl.ds(step * TOTAL_GROUP, TOTAL_GROUP)
-        return pltpu.make_async_copy(expo_buf.at[span], expo_hbm.at[span], expo_sem.at[step])
-
-    row = lax.broadcasted_iota(jnp.int32, (nk_buf.shape[1], code_ref.shape[1]), 0)
+    row = lax.broadcasted_iota(jnp.int32, expo_ref.shape[1:], 0)
 
     def first():
         out_ref[...] = jnp.zeros_like(out_ref)
 
     def body(p, slot):
-        raw = products(nk_buf[slot], q_buf[slot])
+        raw = products(nk_buf[slot], q_ref[p])
         code = code_ref[pl.ds(pair_query[p], 1), :]
         expo = jnp.where(row < count[pair_tile[p]], jnp.exp2(raw * log2_scale), 0.0)
-        expo_buf[p] = expo
+        expo_ref[p] = expo
         total = jnp.sum(expo, axis=0, keepdims=True)
         picked = jnp.sum(jnp.where(row == code, raw, 0.0), axis=0, keepdims=True)
         out_ref[pl.ds(pair_out[p], 1), :] = jnp.where(code > -2, total, 0.0)
-        out_ref[pl.ds(pair_out[p] + slots, 1), :] = picked * inv_temp
-
-    sources = [(nk_hbm, pair_tile, nk_buf, nk_sem), (q_hbm, pair_query, q_buf, q_sem)]
-    send = lambda step: part(step).start()
-    groups = over_pairs(pairs[0], TOTAL_GROUP, sources, first, body, send)
-
-    @pl.loop(0, groups)
-    def _(step):
-        part(step).wait()
+        out_ref[pl.ds(pair_out[p] + half, 1), :] = picked * inv_temp
+
+    sources = [
+        (nk_hbm, pair_tile, nk_buf, nk_sem, True),
+        (q_hbm, pair_query, q_ref, q_sem, False),
+    ]
+    over_pairs(pairs[0], TOTAL_GROUP, TOTAL_AHEAD, sources, first, body)
+
+
+def share_kernel(arrived_ref, scale_ref, loss_ref):
+    half = loss_ref.shape[0]
+    sums = jnp.sum(arrived_ref[...], axis=0)
+    total = sums[:half]
+    loss_ref[...] = jnp.log(total) - sums[half:]
+    scale_ref[...] = jnp.broadcast_to((1.0 / total)[None], scale_ref.shape)
 
 
 def grad_kernel(
-    pair_tile, pair_query, pairs, expo_hbm, q_hbm, code_ref, scale_ref, out_hbm,
-    expo_buf, q_buf, expo_sem, q_sem, sum_buf, out_buf, out_sem, sent,
+    pair_tile, pair_query, pairs, expo_ref, q_ref, code_ref, scale_ref, out_hbm,
+    sum_buf, out_buf, out_sem, sent,
 ):
-    row = lax.broadcasted_iota(jnp.int32, expo_buf.shape[1:], 0)
+    row = lax.broadcasted_iota(jnp.int32, expo_ref.shape[1:], 0)
     most = pair_tile.shape[0]
     tiles = out_hbm.shape[0]
 
@@ -137,8 +139,8 @@
         code = code_ref[pl.ds(query, 1), :]
         scale = jnp.where(code > -2, scale_ref[pl.ds(query, 1), :], 0.0)
         target = jnp.where(row == code, 1.0, 0.0)
-        weights = (expo_buf[slot] * scale - target).astype(jnp.bfloat16)
-        grad = jnp.dot(weights, q_buf[slot], preferred_element_type=jnp.float32)
+        weights = (expo_ref[p] * scale - target).astype(jnp.bfloat16)
+        grad = jnp.dot(weights, q_ref[p], preferred_element_type=jnp.float32)
         same = pair_tile[jnp.maximum(p - 1, 0)] == tile
         grad = jnp.where(same, sum_buf[...], 0.0) + grad
         sum_buf[...] = grad
@@ -148,8 +150,7 @@
         ahead = (step + 1) * GRAD_GROUP
         send_until(jnp.where(ahead < pairs[0], pair_tile[jnp.minimum(ahead, most - 1)], 0))
 
-    sources = [(expo_hbm, None, expo_buf, expo_sem), (q_hbm, pair_query, q_buf, q_sem)]
-    over_pairs(pairs[0], GRAD_GROUP, sources, first, body, last)
+    over_pairs(pairs[0], GRAD_GROUP, 0, [], first, body, last)
     send_until(tiles)
 
     @pl.loop(0, tiles // OUT_GROUP)
@@ -157,26 +158,20 @@
         part(group).wait()
 
 
-def tile_call(kernel, scalars, blocks, tables, out_shape, out_spaces, slots, wide, name):
-    smem, vmem, hbm = (pl.BlockSpec(memory_space=m) for m in (pltpu.SMEM, pltpu.VMEM, pl.ANY))
-    most = scalars[0].shape[0]
-    rows, width = blocks[1].shape[1:]
-    scratch = [pltpu.VMEM((slots,) + block.shape[1:], block.dtype) for block in blocks]
-    scratch += [pltpu.SemaphoreType.DMA((slots,)) for block in blocks]
+def tile_call(kernel, operands, out_shape, out_spaces, scratch, vmem_mib, name):
     return pl.pallas_call(
         kernel,
-        in_specs=[smem] * len(scalars) + [hbm] * len(blocks) + [vmem] * len(tables),
-        out_specs=[pl.BlockSpec(memory_space=m) for m in out_spaces],
+        in_specs=[pl.BlockSpec(memory_space=space) for space, _ in operands],
+        out_specs=[pl.BlockSpec(memory_space=space) for space in out_spaces],
         out_shape=out_shape,
-        scratch_shapes=scratch + wide,
-        cost_estimate=pl.CostEstimate(
-            flops=2 * most * rows * rows * width,
-            bytes_accessed=4 * most * rows * width,
-            transcendentals=most * rows * rows,
-        ),
-        compiler_params=pltpu.CompilerParams(vmem_limit_bytes=58 * 1024 * 1024),
+        scratch_shapes=scratch,
+        compiler_params=pltpu.CompilerParams(vmem_limit_bytes=vmem_mib * 1024 * 1024),
         name=name,
-    )(*scalars, *blocks, *tables)
+    )(*[x for _, x in operands])
+
+
+def in_space(space, arrays):
+    return [(space, x) for x in arrays]
 
 
 def pair_lists(code, key_dest, query_tiles):
@@ -225,40 +220,55 @@
     pair_tile, pair_query, pair_out, pairs = pair_lists(code, key_dest, query_tiles)
     code = code.reshape(devices * query_tiles, rows)
     most = pair_tile.shape[0]
-    expo_shape = jax.ShapeDtypeStruct((most, rows, rows), jnp.float32)
-    partial, expo = tile_call(
+    slots = (TOTAL_AHEAD + 1) * TOTAL_GROUP
+    partial, expo, picks = tile_call(
         functools.partial(total_kernel, query_tiles),
-        [pair_tile, pair_query, pair_out, pairs, key_count],
-        [nk, queries],
-        [code],
-        [jax.ShapeDtypeStruct((devices * 2 * query_tiles, rows), jnp.float32), expo_shape],
-        [pltpu.VMEM, pl.ANY],
-        4 * TOTAL_GROUP,
-        [
-            pltpu.VMEM(expo_shape.shape, jnp.float32),
-            pltpu.SemaphoreType.DMA((most // TOTAL_GROUP,)),
-        ],
+        in_space(pltpu.SMEM, [pair_tile, pair_query, pair_out, pairs, key_count])
+        + in_space(pl.ANY, [nk, queries])
+        + in_space(pltpu.VMEM, [code]),
+        [
+            jax.ShapeDtypeStruct((devices * 2 * query_tiles, rows), jnp.float32),
+            pltpu.VMEM((most, rows, rows), jnp.float32),
+            pltpu.VMEM((most, rows, width), jnp.bfloat16),
+        ],
+        [pltpu.VMEM] * 3,
+        [
+            pltpu.VMEM((slots, rows, width), jnp.bfloat16),
+            pltpu.SemaphoreType.DMA((slots,)),
+            pltpu.SemaphoreType.DMA((slots,)),
+        ],
+        TOTAL_MIB,
         "totals",
     )
+    expo = pltpu.with_memory_space_constraint(expo, pltpu.VMEM)
+    picks = pltpu.with_memory_space_constraint(picks, pltpu.VMEM)
     partial = partial.reshape(devices, 2 * query_tiles, rows)
-    arrived = jnp.sum(exchange(partial), axis=0)
-    total, picked = arrived[:query_tiles], arrived[query_tiles:]
-    scale = exchange(jnp.broadcast_to((1.0 / total)[None], (devices, query_tiles, rows)))
-    loss = jnp.log(total) - picked
+    scale, loss = tile_call(
+        share_kernel,
+        in_space(pltpu.VMEM, [exchange(partial)]),
+        [
+            jax.ShapeDtypeStruct((devices, query_tiles, rows), jnp.float32),
+            jax.ShapeDtypeStruct((query_tiles, rows), jnp.float32),
+        ],
+        [pltpu.VMEM] * 2,
+        [],
+        SHARE_MIB,
+        "share",
+    )
+    scale = exchange(scale)
     (key_grad,) = tile_call(
         grad_kernel,
-        [pair_tile, pair_query, pairs],
-        [expo, queries],
-        [code, scale.reshape(devices * query_tiles, rows)],
+        in_space(pltpu.SMEM, [pair_tile, pair_query, pairs])
+        + in_space(pltpu.VMEM, [expo, picks, code, scale.reshape(devices * query_tiles, rows)]),
         [jax.ShapeDtypeStruct((tiles, rows, width), jnp.bfloat16)],
         [pl.ANY],
-        5 * GRAD_GROUP,
         [
             pltpu.VMEM((rows, width), jnp.float32),
             pltpu.VMEM((tiles + 1, rows, width), jnp.bfloat16),
             pltpu.SemaphoreType.DMA((tiles // OUT_GROUP,)),
             pltpu.SMEM((1,), jnp.int32),
         ],
+        GRAD_MIB,
         "grads",
     )
     return (loss, key_grad)

time: 190 us -> 191 us (level)
  blocking collectives: 36.9 us -> 41 us
  Pallas kernels: 19.7 us -> 16 us
  local copies, waits for them, and re-layouts: 2.43 us -> 4.59 us
    all_to_all x2, blocking collectives: 36.9 us -> 41 us  [exchange(): return lax.all_to_all(x, AXES, split_axis=0, concat_axis=0, tiled=True)]
    pallas_call x2 -> x3, Pallas kernels: 19.7 us -> 16 us  [tile_call(): pl.pallas_call(kernel, in_specs=[pl.BlockSpec(memory_space=space) for spa...]
    unnamed x7 -> x9, local copies, waits for them, and re-layouts: 0.11 us -> 2.3 us
  transfers between devices with their start and end apart: 3 -> 3, of which waited for: 3 -> 3; matrix products, arithmetic and copies ran while one was open for 10% -> 9% of each run, Pallas kernels for 0% -> 0%
where the time goes in v6:
time: 191 us; the launch traced here: 190 us
  waiting for transfers between devices  74.4 us (39%)
  blocking collectives  41 us (21%)
  starting transfers between devices  20.8 us (11%)
  other arithmetic  18.1 us (9%)
  Pallas kernels  16 us (8%)
  between operations  15.5 us (8%)
  local copies, waits for them, and re-layouts  4.59 us (2%)
    all_gather x1, waiting for transfers between devices, shards(): queries = lax.all_gather(unit_rows(query_feats), AXES, axis=0, tiled=True)  63.8 us
    all_to_all x2, blocking collectives, exchange(): return lax.all_to_all(x, AXES, split_axis=0, concat_axis=0, tiled=True)  41 us
    all_to_all x2, starting transfers between devices, exchange(): return lax.all_to_all(x, AXES, split_axis=0, concat_axis=0, tiled=True)  20.8 us
    pallas_call x3, Pallas kernels, tile_call(): pl.pallas_call(kernel, in_specs=[pl.BlockSpec(memory_space=space) for spa...  16 us
    all_to_all x2, waiting for transfers between devices, exchange(): return lax.all_to_all(x, AXES, split_axis=0, concat_axis=0, tiled=True)  10.6 us
    convert_element_type x2, other arithmetic, unit_rows(): return scaled.astype(jnp.bfloat16)  6.02 us
    reduce_sum x2, other arithmetic, unit_rows(): jnp.mean(xf * xf, axis=-1, keepdims=True) + eps  4.52 us
  transfers between devices with their start and end apart: 3, of which 3 were waited for; matrix products, arithmetic and copies ran while one was open for 9% of the time, Pallas kernels for 0%

profile of v6, /device:TPU:1, one launch (start us, length us, event | category | flops | bytes accessed | tf_op | source)
XLA Modules:
  0.0 190.4 jit_solution(11997784585935911016)
XLA Ops:
  7.2 1.1 fusion.3
  8.4 1.8 fusion.5
  10.2 0.7 broadcast_add_fusion
  10.8 0.7 select_reduce_fusion.7
  11.6 0.7 copy.28
  12.3 11.5 %all-to-all-start = ((s32[128,1,1]{2,1,0:T(1,128)}), s32[128,1,1]{2,1,0:T(1,128)S(1)}, u32[]{:S(2)}, u32[]{:S(2)}) async-start(s32[128,1,1]{2,1,0:T(1,128)} %copy.28), calls=%async_computation | async-start | bytes 131072 | tf_op jit(solution)/shard_map/all_to_all | solution.py:33
  23.8 0.7 broadcast_in_dim.156
  24.7 0.7 and_select_fusion.2
  25.4 3.4 %fusion = f32[64,128]{1,0:T(8,128)S(1)} fusion(bf16[64,128,256]{2,1,0:T(8,128)(2,1)} %param.7), kind=kLoop, calls=%fused_computation.2 | loop fusion | flops 6283264 | bytes 4227072 | tf_op jit(solution)/shard_map/reduce_sum | solution.py:27
  28.8 4.2 %fusion.2.nk_hbm = bf16[64,128,256]{2,1,0:T(8,128)(2,1)} fusion(bf16[64,128,256]{2,1,0:T(8,128)(2,1)} %param.7, f32[64,128]{1,0:T(8,128)S(1)} %add_rsqrt_fusion), kind=kLoop, calls=%fused_computation.4 | loop fusion | flops 8388608 | bytes 8421376 | tf_op jit(solution)/shard_map/convert_element_type | solution.py:29
  33.5 2.3 %reduce.2 = s32[128]{0:T(128)S(1)} reduce(s32[128,1,1]{2,1,0:T(1,128)S(1)} %all-to-all-done, s32[]{:T(128)} %constant.61.clone.1), dimensions={1,2}, to_apply=%all_to_all.12.reduce_sub_computation | reduce | bytes 1028 | tf_op jit(solution)/shard_map/all_to_all | solution.py:33
  36.0 1.0 broadcast_select_fusion
  37.1 9.3 %all-to-all-start.1 = ((s32[128,4,128]{2,1,0:T(4,128)}), s32[128,4,128]{2,1,0:T(4,128)S(1)}, u32[]{:S(2)}, u32[]{:S(2)}) async-start(s32[128,4,128]{2,1,0:T(4,128)} %broadcast_select_fusion), calls=%async_computation.1 | async-start | bytes 524288 | tf_op jit(solution)/shard_map/all_to_all | solution.py:33
  46.4 0.5 slice.8
  48.3 10.2 %all-to-all-done.1 = s32[128,4,128]{2,1,0:T(4,128)S(1)} async-done(((s32[128,4,128]{2,1,0:T(4,128)}), s32[128,4,128]{2,1,0:T(4,128)S(1)}, u32[]{:S(2)}, u32[]{:S(2)}) %all-to-all-start.1) | async-done | bytes 262176 | tf_op jit(solution)/shard_map/all_to_all | solution.py:33
  58.6 0.8 select_reduce_fusion.4
  59.9 0.6 fusion.9
  60.6 63.8 %all-gather.2.cloned.1.call-done.q_hbm = bf16[512,128,256]{2,1,0:T(8,128)(2,1)} async-done(((bf16[4,128,256]{2,1,0:T(8,128)(2,1)}), bf16[512,128,256]{2,1,0:T(8,128)(2,1)}) %all-gather.2.cloned.1.call-update) | async-done | bytes 33554448 | tf_op jit(solution)/shard_map/all_gather | solution.py:204
  124.4 2.2 %copy-done = bf16[64,128,256]{2,1,0:T(8,128)(2,1)S(1)} copy-done((bf16[64,128,256]{2,1,0:T(8,128)(2,1)S(1)}, bf16[64,128,256]{2,1,0:T(8,128)(2,1)}, u32[]{:S(2)}) %copy-start) | copy-done | bytes 4194328
  126.5 10.5 %totals.1 = (f32[1024,128]{1,0:T(8,128)S(1)}, f32[256,128,128]{2,1,0:T(8,128)S(1)}, bf16[256,128,256]{2,1,0:T(8,128)(2,1)S(1)}) custom-call(s32[256]{0:T(256)S(1)} %get-tuple-element.16.pair_tile, s32[256]{0:T(256)S(1)} %get-tuple-element.20.pair_query, s32[256]{0:T(256)S(1)} %get-tuple-element.19.pair_out, s32[1]{0:T(128)} %bitcast.4.pairs, ...), custom_call_target="tpu_custom_call" | custom-call | tf_op jit(solution)/shard_map/totals/pallas_call | solution.py:162
  137.0 25.8 %all_to_all.20.arrived_ref = f32[128,8,128]{2,1,0:T(8,128)S(1)} all-to-all(f32[128,8,128]{2,1,0:T(8,128)S(1)} %bitcast.14), channel_id=1, replica_groups=mesh['cam'=32,'lidar'=4] {'cam','lidar'}, dimensions={0} | all-to-all | bytes 1048576 | tf_op jit(solution)/shard_map/all_to_all | solution.py:33
  162.8 0.8 share.1
  163.5 15.2 %all_to_all.21 = f32[128,4,128]{2,1,0:T(4,128)S(1)} all-to-all(f32[128,4,128]{2,1,0:T(4,128)S(1)} %get-tuple-element.11), channel_id=1, replica_groups=mesh['cam'=32,'lidar'=4] {'cam','lidar'}, dimensions={0} | all-to-all | bytes 524288 | tf_op jit(solution)/shard_map/all_to_all | solution.py:33
  178.8 4.8 %grads.1 = bf16[64,128,256]{2,1,0:T(8,128)(2,1)} custom-call(s32[256]{0:T(256)S(1)} %get-tuple-element.16.pair_tile, s32[256]{0:T(256)S(1)} %get-tuple-element.20.pair_query, s32[1]{0:T(128)} %bitcast.4.pairs, f32[256,128,128]{2,1,0:T(8,128)S(1)} %get-tuple-element.9.expo_ref, bf16[256,128,256]{2,1,0:T(8,128)(2,1)S(1)} %get-tuple-element.10.q_ref, ...), custom_call_target="tpu_custom_call" | custom-call | tf_op jit(solution)/shard_map/grads/pallas_call | solution.py:162
  (26 shorter events, 1.6 us)
Async XLA Ops:
  7.2 41.0 %copy-start.3 = (s32[64]{0:T(128)S(1)}, s32[64]{0:T(128)}, u32[]{:S(2)}) copy-start(s32[64]{0:T(128)} %param.9) | copy-start | bytes 772
  7.2 28.8 %copy-start.2 = (s32[4,128]{1,0:T(4,128)S(1)}, s32[4,128]{1,0:T(4,128)}, u32[]{:S(2)}) copy-start(s32[4,128]{1,0:T(4,128)} %param.13) | copy-start | bytes 6148
  7.2 117.2 %copy-start.1 = (s32[64]{0:T(128)S(1)}, s32[64]{0:T(128)}, u32[]{:S(2)}) copy-start(s32[64]{0:T(128)} %count.1) | copy-start | bytes 772
  7.2 117.2 %all-gather.2.cloned.1.call-start = ((), (), s32[]{:S(2)}) async-start(), calls=%async_computation.4 | async-start | bytes 33816576 | tf_op jit(solution)/shard_map/all_gather | solution.py:204
  12.3 21.1 %all-to-all-start = ((s32[128,1,1]{2,1,0:T(1,128)}), s32[128,1,1]{2,1,0:T(1,128)S(1)}, u32[]{:S(2)}, u32[]{:S(2)}) async-start(s32[128,1,1]{2,1,0:T(1,128)} %copy.28), calls=%async_computation | async-start | bytes 131072 | tf_op jit(solution)/shard_map/all_to_all | solution.py:33
  37.1 21.4 %all-to-all-start.1 = ((s32[128,4,128]{2,1,0:T(4,128)}), s32[128,4,128]{2,1,0:T(4,128)S(1)}, u32[]{:S(2)}, u32[]{:S(2)}) async-start(s32[128,4,128]{2,1,0:T(4,128)} %broadcast_select_fusion), calls=%async_computation.1 | async-start | bytes 524288 | tf_op jit(solution)/shard_map/all_to_all | solution.py:33
  124.3 2.2 %copy-start = (bf16[64,128,256]{2,1,0:T(8,128)(2,1)S(1)}, bf16[64,128,256]{2,1,0:T(8,128)(2,1)}, u32[]{:S(2)}) copy-start(bf16[64,128,256]{2,1,0:T(8,128)(2,1)} %fusion.2.nk_hbm) | copy-start | bytes 12582916
Sparse Core Ops, SparseCore 0:
  11.2 113.1 all-gather.1

commit v7 on v6

--- a/solution.py
+++ b/solution.py
@@ -216,7 +216,7 @@
     )
     code = exchange(code)
 
-    nk = unit_rows(key_feats)
+    nk = pltpu.with_memory_space_constraint(unit_rows(key_feats), pltpu.HBM)
     pair_tile, pair_query, pair_out, pairs = pair_lists(code, key_dest, query_tiles)
     code = code.reshape(devices * query_tiles, rows)
     most = pair_tile.shape[0]

time: 191 us -> 182 us (0.953)
  blocking collectives: 41 us -> 35.5 us
  local copies, waits for them, and re-layouts: 4.59 us -> 2.4 us
    all_to_all x2, blocking collectives: 41 us -> 35.5 us  [exchange(): return lax.all_to_all(x, AXES, split_axis=0, concat_axis=0, tiled=True)]
    unnamed x9 -> x7, local copies, waits for them, and re-layouts: 2.3 us -> 0.11 us
  transfers between devices with their start and end apart: 3 -> 3, of which waited for: 3 -> 3; matrix products, arithmetic and copies ran while one was open for 9% -> 10% of each run, Pallas kernels for 0% -> 0%
where the time goes in v7:
time: 182 us
  waiting for transfers between devices  74.4 us (41%)
  blocking collectives  35.5 us (20%)
  starting transfers between devices  20.8 us (11%)
  other arithmetic  18.1 us (10%)
  between operations  15.5 us (9%)
  Pallas kernels  15 us (8%)
  local copies, waits for them, and re-layouts  2.4 us (1%)
    all_gather x1, waiting for transfers between devices, shards(): queries = lax.all_gather(unit_rows(query_feats), AXES, axis=0, tiled=True)  63.8 us
    all_to_all x2, blocking collectives, exchange(): return lax.all_to_all(x, AXES, split_axis=0, concat_axis=0, tiled=True)  35.5 us
    all_to_all x2, starting transfers between devices, exchange(): return lax.all_to_all(x, AXES, split_axis=0, concat_axis=0, tiled=True)  20.8 us
    pallas_call x3, Pallas kernels, tile_call(): pl.pallas_call(kernel, in_specs=[pl.BlockSpec(memory_space=space) for spa...  15 us
    all_to_all x2, waiting for transfers between devices, exchange(): return lax.all_to_all(x, AXES, split_axis=0, concat_axis=0, tiled=True)  10.6 us
    convert_element_type x2, other arithmetic, unit_rows(): return scaled.astype(jnp.bfloat16)  6.02 us
    reduce_sum x2, other arithmetic, unit_rows(): jnp.mean(xf * xf, axis=-1, keepdims=True) + eps  4.52 us
  transfers between devices with their start and end apart: 3, of which 3 were waited for; matrix products, arithmetic and copies ran while one was open for 10% of the time, Pallas kernels for 0%

profile of v7, /device:TPU:1, one launch (start us, length us, event | category | flops | bytes accessed | tf_op | source)
XLA Modules:
  0.0 181.8 jit_solution(1149553088746064455)
XLA Ops:
  7.2 1.1 fusion.3
  8.4 1.8 fusion.5
  10.2 0.7 broadcast_add_fusion
  10.8 0.7 select_reduce_fusion.7
  11.6 0.7 copy.28
  12.3 11.5 %all-to-all-start = ((s32[128,1,1]{2,1,0:T(1,128)}), s32[128,1,1]{2,1,0:T(1,128)S(1)}, u32[]{:S(2)}, u32[]{:S(2)}) async-start(s32[128,1,1]{2,1,0:T(1,128)} %copy.28), calls=%async_computation | async-start | bytes 131072 | tf_op jit(solution)/shard_map/all_to_all | solution.py:33
  23.8 0.7 broadcast_in_dim.156
  24.7 0.7 and_select_fusion.2
  25.4 3.4 %fusion = f32[64,128]{1,0:T(8,128)S(1)} fusion(bf16[64,128,256]{2,1,0:T(8,128)(2,1)} %param.7), kind=kLoop, calls=%fused_computation.2 | loop fusion | flops 6283264 | bytes 4227072 | tf_op jit(solution)/shard_map/reduce_sum | solution.py:27
  28.8 4.2 %fusion.2.nk_hbm = bf16[64,128,256]{2,1,0:T(8,128)(2,1)} fusion(bf16[64,128,256]{2,1,0:T(8,128)(2,1)} %param.7, f32[64,128]{1,0:T(8,128)S(1)} %add_rsqrt_fusion), kind=kLoop, calls=%fused_computation.4 | loop fusion | flops 8388608 | bytes 8421376 | tf_op jit(solution)/shard_map/convert_element_type | solution.py:29
  33.0 0.4 all-to-all-done
  33.5 2.3 %reduce.2 = s32[128]{0:T(128)S(1)} reduce(s32[128,1,1]{2,1,0:T(1,128)S(1)} %all-to-all-done, s32[]{:T(128)} %constant.61.clone.1), dimensions={1,2}, to_apply=%all_to_all.12.reduce_sub_computation | reduce | bytes 1028 | tf_op jit(solution)/shard_map/all_to_all | solution.py:33
  36.0 1.0 broadcast_select_fusion
  37.1 9.3 %all-to-all-start.1 = ((s32[128,4,128]{2,1,0:T(4,128)}), s32[128,4,128]{2,1,0:T(4,128)S(1)}, u32[]{:S(2)}, u32[]{:S(2)}) async-start(s32[128,4,128]{2,1,0:T(4,128)} %broadcast_select_fusion), calls=%async_computation.1 | async-start | bytes 524288 | tf_op jit(solution)/shard_map/all_to_all | solution.py:33
  46.4 0.5 slice.8
  48.3 10.2 %all-to-all-done.1 = s32[128,4,128]{2,1,0:T(4,128)S(1)} async-done(((s32[128,4,128]{2,1,0:T(4,128)}), s32[128,4,128]{2,1,0:T(4,128)S(1)}, u32[]{:S(2)}, u32[]{:S(2)}) %all-to-all-start.1) | async-done | bytes 262176 | tf_op jit(solution)/shard_map/all_to_all | solution.py:33
  58.6 0.8 select_reduce_fusion.4
  59.9 0.6 fusion.9
  60.6 63.8 %all-gather.2.cloned.1.call-done.q_hbm = bf16[512,128,256]{2,1,0:T(8,128)(2,1)} async-done(((bf16[4,128,256]{2,1,0:T(8,128)(2,1)}), bf16[512,128,256]{2,1,0:T(8,128)(2,1)}) %all-gather.2.cloned.1.call-update) | async-done | bytes 33554448 | tf_op jit(solution)/shard_map/all_gather | solution.py:204
  124.3 8.6 %totals.1 = (f32[1024,128]{1,0:T(8,128)S(1)}, f32[256,128,128]{2,1,0:T(8,128)S(1)}, bf16[256,128,256]{2,1,0:T(8,128)(2,1)S(1)}) custom-call(s32[256]{0:T(256)S(1)} %get-tuple-element.16.pair_tile, s32[256]{0:T(256)S(1)} %get-tuple-element.20.pair_query, s32[256]{0:T(256)S(1)} %get-tuple-element.19.pair_out, s32[1]{0:T(128)} %bitcast.4.pairs, s32[64]{0:T(128)S(1)} %copy-done, ...), custom_call_target="tpu_custom_call" | custom-call | tf_op jit(solution)/shard_map/totals/pallas_call | solution.py:162
  133.0 20.3 %all_to_all.20.arrived_ref = f32[128,8,128]{2,1,0:T(8,128)S(1)} all-to-all(f32[128,8,128]{2,1,0:T(8,128)S(1)} %bitcast.14), channel_id=1, replica_groups=mesh['cam'=32,'lidar'=4] {'cam','lidar'}, dimensions={0} | all-to-all | bytes 1048576 | tf_op jit(solution)/shard_map/all_to_all | solution.py:33
  153.3 0.8 share.1
  154.0 15.2 %all_to_all.21 = f32[128,4,128]{2,1,0:T(4,128)S(1)} all-to-all(f32[128,4,128]{2,1,0:T(4,128)S(1)} %get-tuple-element.11), channel_id=1, replica_groups=mesh['cam'=32,'lidar'=4] {'cam','lidar'}, dimensions={0} | all-to-all | bytes 524288 | tf_op jit(solution)/shard_map/all_to_all | solution.py:33
  169.2 5.7 %grads.1 = bf16[64,128,256]{2,1,0:T(8,128)(2,1)} custom-call(s32[256]{0:T(256)S(1)} %get-tuple-element.16.pair_tile, s32[256]{0:T(256)S(1)} %get-tuple-element.20.pair_query, s32[1]{0:T(128)} %bitcast.4.pairs, f32[256,128,128]{2,1,0:T(8,128)S(1)} %get-tuple-element.9.expo_ref, bf16[256,128,256]{2,1,0:T(8,128)(2,1)S(1)} %get-tuple-element.10.q_ref, ...), custom_call_target="tpu_custom_call" | custom-call | tf_op jit(solution)/shard_map/grads/pallas_call | solution.py:162
  (24 shorter events, 1.1 us)
Async XLA Ops:
  7.2 41.0 %copy-start.2 = (s32[64]{0:T(128)S(1)}, s32[64]{0:T(128)}, u32[]{:S(2)}) copy-start(s32[64]{0:T(128)} %param.9) | copy-start | bytes 772
  7.2 28.8 %copy-start.1 = (s32[4,128]{1,0:T(4,128)S(1)}, s32[4,128]{1,0:T(4,128)}, u32[]{:S(2)}) copy-start(s32[4,128]{1,0:T(4,128)} %param.13) | copy-start | bytes 6148
  7.2 117.2 %copy-start = (s32[64]{0:T(128)S(1)}, s32[64]{0:T(128)}, u32[]{:S(2)}) copy-start(s32[64]{0:T(128)} %count.1) | copy-start | bytes 772
  7.2 117.2 %all-gather.2.cloned.1.call-start = ((), (), s32[]{:S(2)}) async-start(), calls=%async_computation.4 | async-start | bytes 33816576 | tf_op jit(solution)/shard_map/all_gather | solution.py:204
  12.3 21.1 %all-to-all-start = ((s32[128,1,1]{2,1,0:T(1,128)}), s32[128,1,1]{2,1,0:T(1,128)S(1)}, u32[]{:S(2)}, u32[]{:S(2)}) async-start(s32[128,1,1]{2,1,0:T(1,128)} %copy.28), calls=%async_computation | async-start | bytes 131072 | tf_op jit(solution)/shard_map/all_to_all | solution.py:33
  37.1 21.4 %all-to-all-start.1 = ((s32[128,4,128]{2,1,0:T(4,128)}), s32[128,4,128]{2,1,0:T(4,128)S(1)}, u32[]{:S(2)}, u32[]{:S(2)}) async-start(s32[128,4,128]{2,1,0:T(4,128)} %broadcast_select_fusion), calls=%async_computation.1 | async-start | bytes 524288 | tf_op jit(solution)/shard_map/all_to_all | solution.py:33
Sparse Core Ops, SparseCore 0:
  11.2 113.1 all-gather.1

commit v8 on v7

--- a/solution.py
+++ b/solution.py
@@ -13,7 +13,7 @@
 eps = 1e-06
 TOTAL_GROUP = 8
 TOTAL_AHEAD = 3
-GRAD_GROUP = 8
+GRAD_GROUP = 16
 OUT_GROUP = 8
 TOTAL_MIB = 5
 GRAD_MIB = 5
@@ -39,16 +39,15 @@
     )
 
 
-def over_pairs(pairs, group, ahead, sources, first, body, last=None):
+def over_pairs(pairs, group, ahead, sources, first, body, last=None, need=None):
     groups = (pairs + (group - 1)) // group
 
     def fetch(step, act):
         base = lax.rem(step, ahead + 1) * group
         for j in range(group):
             p = step * group + j
-            for hbm, index, buf, sem, ring in sources:
-                place = buf.at[base + j if ring else p]
-                act(pltpu.make_async_copy(hbm.at[index[p]], place, sem.at[base + j]))
+            for hbm, index, buf, sem in sources:
+                act(pltpu.make_async_copy(hbm.at[index[p]], buf.at[p], sem.at[base + j]))
 
     start = lambda copy: copy.start()
     for early in range(ahead):
@@ -66,24 +65,49 @@
             fetch(step + ahead, start)
 
         fetch(step, lambda copy: copy.wait())
-        base = lax.rem(step, ahead + 1) * group
+        if need is not None:
+            need(step)
         for j in range(group):
-            body(step * group + j, base + j)
+            body(step * group + j)
         if last is not None:
             last(step)
 
 
 def total_kernel(
     half, pair_tile, pair_query, pair_out, pairs, count, nk_hbm, q_hbm, code_ref,
-    out_ref, expo_ref, q_ref, nk_buf, nk_sem, q_sem,
+    out_ref, expo_ref, q_ref, nk_buf, nk_sem, q_sem, held,
 ):
     row = lax.broadcasted_iota(jnp.int32, expo_ref.shape[1:], 0)
 
+    chunks = nk_buf.shape[0] // OUT_GROUP
+
+    def chunk(index):
+        span = pl.ds(index * OUT_GROUP, OUT_GROUP)
+        return pltpu.make_async_copy(nk_hbm.at[span], nk_buf.at[span], nk_sem.at[index])
+
+    def hold_until(most):
+        ready = jnp.maximum(most, held[0])
+
+        @pl.loop(held[0], ready)
+        def _(index):
+            chunk(index).wait()
+
+        held[0] = ready
+
     def first():
+        for index in range(1, chunks):
+            chunk(index).start()
         out_ref[...] = jnp.zeros_like(out_ref)
 
-    def body(p, slot):
-        raw = products(nk_buf[slot], q_ref[p])
+    def need(step):
+        final = jnp.minimum((step + 1) * TOTAL_GROUP, pairs[0]) - 1
+        hold_until(pair_tile[final] // OUT_GROUP + 1)
+
+    held[0] = 0
+    chunk(0).start()
+
+    def body(p):
+        raw = products(nk_buf[pair_tile[p]], q_ref[p])
         code = code_ref[pl.ds(pair_query[p], 1), :]
         expo = jnp.where(row < count[pair_tile[p]], jnp.exp2(raw * log2_scale), 0.0)
         expo_ref[p] = expo
@@ -92,11 +116,9 @@
         out_ref[pl.ds(pair_out[p], 1), :] = jnp.where(code > -2, total, 0.0)
         out_ref[pl.ds(pair_out[p] + half, 1), :] = picked * inv_temp
 
-    sources = [
-        (nk_hbm, pair_tile, nk_buf, nk_sem, True),
-        (q_hbm, pair_query, q_ref, q_sem, False),
-    ]
-    over_pairs(pairs[0], TOTAL_GROUP, TOTAL_AHEAD, sources, first, body)
+    sources = [(q_hbm, pair_query, q_ref, q_sem)]
+    over_pairs(pairs[0], TOTAL_GROUP, TOTAL_AHEAD, sources, first, body, need=need)
+    hold_until(chunks)
 
 
 def share_kernel(arrived_ref, scale_ref, loss_ref):
@@ -133,7 +155,7 @@
         sum_buf[...] = jnp.zeros_like(sum_buf)
         sent[0] = 0
 
-    def body(p, slot):
+    def body(p):
         valid = p < pairs[0]
         tile, query = pair_tile[p], pair_query[p]
         code = code_ref[pl.ds(query, 1), :]
@@ -233,9 +255,10 @@
         ],
         [pltpu.VMEM] * 3,
         [
-            pltpu.VMEM((slots, rows, width), jnp.bfloat16),
+            pltpu.VMEM((tiles, rows, width), jnp.bfloat16),
+            pltpu.SemaphoreType.DMA((tiles // OUT_GROUP,)),
             pltpu.SemaphoreType.DMA((slots,)),
-            pltpu.SemaphoreType.DMA((slots,)),
+            pltpu.SMEM((1,), jnp.int32),
         ],
         TOTAL_MIB,
         "totals",

time: 182 us -> 181 us (level)
  Pallas kernels: 15 us -> 11.1 us
  blocking collectives: 35.5 us -> 37.7 us
    pallas_call x3, Pallas kernels: 15 us -> 11.1 us  [tile_call(): pl.pallas_call(kernel, in_specs=[pl.BlockSpec(memory_space=space) for spa...]
    all_to_all x2, blocking collectives: 35.5 us -> 37.7 us  [exchange(): return lax.all_to_all(x, AXES, split_axis=0, concat_axis=0, tiled=True)]
where the time goes in v8:
time: 181 us; the launch traced here: 180 us
  waiting for transfers between devices  74.4 us (41%)
  blocking collectives  37.7 us (21%)
  starting transfers between devices  20.8 us (11%)
  other arithmetic  18.1 us (10%)
  between operations  15.5 us (9%)
  Pallas kernels  11.1 us (6%)
  local copies, waits for them, and re-layouts  2.4 us (1%)
    all_gather x1, waiting for transfers between devices, shards(): queries = lax.all_gather(unit_rows(query_feats), AXES, axis=0, tiled=True)  63.8 us
    all_to_all x2, blocking collectives, exchange(): return lax.all_to_all(x, AXES, split_axis=0, concat_axis=0, tiled=True)  37.7 us
    all_to_all x2, starting transfers between devices, exchange(): return lax.all_to_all(x, AXES, split_axis=0, concat_axis=0, tiled=True)  20.8 us
    pallas_call x3, Pallas kernels, tile_call(): pl.pallas_call(kernel, in_specs=[pl.BlockSpec(memory_space=space) for spa...  11.1 us
    all_to_all x2, waiting for transfers between devices, exchange(): return lax.all_to_all(x, AXES, split_axis=0, concat_axis=0, tiled=True)  10.6 us
    convert_element_type x2, other arithmetic, unit_rows(): return scaled.astype(jnp.bfloat16)  6.02 us
    reduce_sum x2, other arithmetic, unit_rows(): jnp.mean(xf * xf, axis=-1, keepdims=True) + eps  4.52 us
  transfers between devices with their start and end apart: 3, of which 3 were waited for; matrix products, arithmetic and copies ran while one was open for 10% of the time, Pallas kernels for 0%

profile of v8, /device:TPU:1, one launch (start us, length us, event | category | flops | bytes accessed | tf_op | source)
XLA Modules:
  0.0 179.9 jit_solution(5904617065305106685)
XLA Ops:
  7.2 1.1 fusion.3
  8.4 1.8 fusion.5
  10.2 0.7 broadcast_add_fusion
  10.8 0.7 select_reduce_fusion.7
  11.6 0.7 copy.28
  12.3 11.5 %all-to-all-start = ((s32[128,1,1]{2,1,0:T(1,128)}), s32[128,1,1]{2,1,0:T(1,128)S(1)}, u32[]{:S(2)}, u32[]{:S(2)}) async-start(s32[128,1,1]{2,1,0:T(1,128)} %copy.28), calls=%async_computation | async-start | bytes 131072 | tf_op jit(solution)/shard_map/all_to_all | solution.py:33
  23.8 0.7 broadcast_in_dim.156
  24.7 0.7 and_select_fusion.2
  25.4 3.4 %fusion = f32[64,128]{1,0:T(8,128)S(1)} fusion(bf16[64,128,256]{2,1,0:T(8,128)(2,1)} %param.7), kind=kLoop, calls=%fused_computation.2 | loop fusion | flops 6283264 | bytes 4227072 | tf_op jit(solution)/shard_map/reduce_sum | solution.py:27
  28.8 4.2 %fusion.2.nk_hbm = bf16[64,128,256]{2,1,0:T(8,128)(2,1)} fusion(bf16[64,128,256]{2,1,0:T(8,128)(2,1)} %param.7, f32[64,128]{1,0:T(8,128)S(1)} %add_rsqrt_fusion), kind=kLoop, calls=%fused_computation.4 | loop fusion | flops 8388608 | bytes 8421376 | tf_op jit(solution)/shard_map/convert_element_type | solution.py:29
  33.0 0.4 all-to-all-done
  33.5 2.3 %reduce.2 = s32[128]{0:T(128)S(1)} reduce(s32[128,1,1]{2,1,0:T(1,128)S(1)} %all-to-all-done, s32[]{:T(128)} %constant.61.clone.1), dimensions={1,2}, to_apply=%all_to_all.12.reduce_sub_computation | reduce | bytes 1028 | tf_op jit(solution)/shard_map/all_to_all | solution.py:33
  36.0 1.0 broadcast_select_fusion
  37.1 9.3 %all-to-all-start.1 = ((s32[128,4,128]{2,1,0:T(4,128)}), s32[128,4,128]{2,1,0:T(4,128)S(1)}, u32[]{:S(2)}, u32[]{:S(2)}) async-start(s32[128,4,128]{2,1,0:T(4,128)} %broadcast_select_fusion), calls=%async_computation.1 | async-start | bytes 524288 | tf_op jit(solution)/shard_map/all_to_all | solution.py:33
  46.4 0.5 slice.8
  48.3 10.2 %all-to-all-done.1 = s32[128,4,128]{2,1,0:T(4,128)S(1)} async-done(((s32[128,4,128]{2,1,0:T(4,128)}), s32[128,4,128]{2,1,0:T(4,128)S(1)}, u32[]{:S(2)}, u32[]{:S(2)}) %all-to-all-start.1) | async-done | bytes 262176 | tf_op jit(solution)/shard_map/all_to_all | solution.py:33
  58.6 0.8 select_reduce_fusion.4
  59.9 0.6 fusion.9
  60.6 63.8 %all-gather.2.cloned.1.call-done.q_hbm = bf16[512,128,256]{2,1,0:T(8,128)(2,1)} async-done(((bf16[4,128,256]{2,1,0:T(8,128)(2,1)}), bf16[512,128,256]{2,1,0:T(8,128)(2,1)}) %all-gather.2.cloned.1.call-update) | async-done | bytes 33554448 | tf_op jit(solution)/shard_map/all_gather | solution.py:226
  124.3 6.0 %totals.1 = (f32[1024,128]{1,0:T(8,128)S(1)}, f32[256,128,128]{2,1,0:T(8,128)S(1)}, bf16[256,128,256]{2,1,0:T(8,128)(2,1)S(1)}) custom-call(s32[256]{0:T(256)S(1)} %get-tuple-element.16.pair_tile, s32[256]{0:T(256)S(1)} %get-tuple-element.20.pair_query, s32[256]{0:T(256)S(1)} %get-tuple-element.19.pair_out, s32[1]{0:T(128)} %bitcast.4.pairs, s32[64]{0:T(128)S(1)} %copy-done, ...), custom_call_target="tpu_custom_call" | custom-call | tf_op jit(solution)/shard_map/totals/pallas_call | solution.py:184
  130.3 22.4 %all_to_all.20.arrived_ref = f32[128,8,128]{2,1,0:T(8,128)S(1)} all-to-all(f32[128,8,128]{2,1,0:T(8,128)S(1)} %bitcast.14), channel_id=1, replica_groups=mesh['cam'=32,'lidar'=4] {'cam','lidar'}, dimensions={0} | all-to-all | bytes 1048576 | tf_op jit(solution)/shard_map/all_to_all | solution.py:33
  152.8 0.8 share.1
  153.5 15.2 %all_to_all.21 = f32[128,4,128]{2,1,0:T(4,128)S(1)} all-to-all(f32[128,4,128]{2,1,0:T(4,128)S(1)} %get-tuple-element.11), channel_id=1, replica_groups=mesh['cam'=32,'lidar'=4] {'cam','lidar'}, dimensions={0} | all-to-all | bytes 524288 | tf_op jit(solution)/shard_map/all_to_all | solution.py:33
  168.7 4.3 %grads.1 = bf16[64,128,256]{2,1,0:T(8,128)(2,1)} custom-call(s32[256]{0:T(256)S(1)} %get-tuple-element.16.pair_tile, s32[256]{0:T(256)S(1)} %get-tuple-element.20.pair_query, s32[1]{0:T(128)} %bitcast.4.pairs, f32[256,128,128]{2,1,0:T(8,128)S(1)} %get-tuple-element.9.expo_ref, bf16[256,128,256]{2,1,0:T(8,128)(2,1)S(1)} %get-tuple-element.10.q_ref, ...), custom_call_target="tpu_custom_call" | custom-call | tf_op jit(solution)/shard_map/grads/pallas_call | solution.py:184
  (24 shorter events, 1.1 us)
Async XLA Ops:
  7.2 41.0 %copy-start.2 = (s32[64]{0:T(128)S(1)}, s32[64]{0:T(128)}, u32[]{:S(2)}) copy-start(s32[64]{0:T(128)} %param.9) | copy-start | bytes 772
  7.2 28.8 %copy-start.1 = (s32[4,128]{1,0:T(4,128)S(1)}, s32[4,128]{1,0:T(4,128)}, u32[]{:S(2)}) copy-start(s32[4,128]{1,0:T(4,128)} %param.13) | copy-start | bytes 6148
  7.2 117.2 %copy-start = (s32[64]{0:T(128)S(1)}, s32[64]{0:T(128)}, u32[]{:S(2)}) copy-start(s32[64]{0:T(128)} %count.1) | copy-start | bytes 772
  7.2 117.2 %all-gather.2.cloned.1.call-start = ((), (), s32[]{:S(2)}) async-start(), calls=%async_computation.4 | async-start | bytes 33816576 | tf_op jit(solution)/shard_map/all_gather | solution.py:226
  12.3 21.1 %all-to-all-start = ((s32[128,1,1]{2,1,0:T(1,128)}), s32[128,1,1]{2,1,0:T(1,128)S(1)}, u32[]{:S(2)}, u32[]{:S(2)}) async-start(s32[128,1,1]{2,1,0:T(1,128)} %copy.28), calls=%async_computation | async-start | bytes 131072 | tf_op jit(solution)/shard_map/all_to_all | solution.py:33
  37.1 21.4 %all-to-all-start.1 = ((s32[128,4,128]{2,1,0:T(4,128)}), s32[128,4,128]{2,1,0:T(4,128)S(1)}, u32[]{:S(2)}, u32[]{:S(2)}) async-start(s32[128,4,128]{2,1,0:T(4,128)} %broadcast_select_fusion), calls=%async_computation.1 | async-start | bytes 524288 | tf_op jit(solution)/shard_map/all_to_all | solution.py:33
Sparse Core Ops, SparseCore 0:
  11.2 113.1 all-gather.1

commit v9 on v8

--- a/solution.py
+++ b/solution.py
@@ -11,8 +11,8 @@
 inv_temp = 1.0 / 0.07
 log2_scale = inv_temp * math.log2(math.e)
 eps = 1e-06
-TOTAL_GROUP = 8
-TOTAL_AHEAD = 3
+TOTAL_GROUP = 16
+TOTAL_AHEAD = 2
 GRAD_GROUP = 16
 OUT_GROUP = 8
 TOTAL_MIB = 5

time: 181 us -> 180 us (level)
  no operation moved by 1% of the time
where the time goes in v9:
time: 180 us
  waiting for transfers between devices  74.4 us (41%)
  blocking collectives  37.5 us (21%)
  starting transfers between devices  20.8 us (12%)
  other arithmetic  18.1 us (10%)
  between operations  15.5 us (9%)
  Pallas kernels  11.4 us (6%)
  local copies, waits for them, and re-layouts  2.4 us (1%)
    all_gather x1, waiting for transfers between devices, shards(): queries = lax.all_gather(unit_rows(query_feats), AXES, axis=0, tiled=True)  63.8 us
    all_to_all x2, blocking collectives, exchange(): return lax.all_to_all(x, AXES, split_axis=0, concat_axis=0, tiled=True)  37.5 us
    all_to_all x2, starting transfers between devices, exchange(): return lax.all_to_all(x, AXES, split_axis=0, concat_axis=0, tiled=True)  20.8 us
    pallas_call x3, Pallas kernels, tile_call(): pl.pallas_call(kernel, in_specs=[pl.BlockSpec(memory_space=space) for spa...  11.4 us
    all_to_all x2, waiting for transfers between devices, exchange(): return lax.all_to_all(x, AXES, split_axis=0, concat_axis=0, tiled=True)  10.6 us
    convert_element_type x2, other arithmetic, unit_rows(): return scaled.astype(jnp.bfloat16)  6.02 us
    reduce_sum x2, other arithmetic, unit_rows(): jnp.mean(xf * xf, axis=-1, keepdims=True) + eps  4.52 us
  transfers between devices with their start and end apart: 3, of which 3 were waited for; matrix products, arithmetic and copies ran while one was open for 10% of the time, Pallas kernels for 0%

profile of v9, /device:TPU:1, one launch (start us, length us, event | category | flops | bytes accessed | tf_op | source)
XLA Modules:
  0.0 180.1 jit_solution(15207856283301671908)
XLA Ops:
  7.2 1.1 fusion.3
  8.4 1.8 fusion.5
  10.2 0.7 broadcast_add_fusion
  10.8 0.7 select_reduce_fusion.7
  11.6 0.7 copy.28
  12.3 11.5 %all-to-all-start = ((s32[128,1,1]{2,1,0:T(1,128)}), s32[128,1,1]{2,1,0:T(1,128)S(1)}, u32[]{:S(2)}, u32[]{:S(2)}) async-start(s32[128,1,1]{2,1,0:T(1,128)} %copy.28), calls=%async_computation | async-start | bytes 131072 | tf_op jit(solution)/shard_map/all_to_all | solution.py:33
  23.8 0.7 broadcast_in_dim.156
  24.7 0.7 and_select_fusion.2
  25.4 3.4 %fusion = f32[64,128]{1,0:T(8,128)S(1)} fusion(bf16[64,128,256]{2,1,0:T(8,128)(2,1)} %param.7), kind=kLoop, calls=%fused_computation.2 | loop fusion | flops 6283264 | bytes 4227072 | tf_op jit(solution)/shard_map/reduce_sum | solution.py:27
  28.8 4.2 %fusion.2.nk_hbm = bf16[64,128,256]{2,1,0:T(8,128)(2,1)} fusion(bf16[64,128,256]{2,1,0:T(8,128)(2,1)} %param.7, f32[64,128]{1,0:T(8,128)S(1)} %add_rsqrt_fusion), kind=kLoop, calls=%fused_computation.4 | loop fusion | flops 8388608 | bytes 8421376 | tf_op jit(solution)/shard_map/convert_element_type | solution.py:29
  33.0 0.4 all-to-all-done
  33.5 2.3 %reduce.2 = s32[128]{0:T(128)S(1)} reduce(s32[128,1,1]{2,1,0:T(1,128)S(1)} %all-to-all-done, s32[]{:T(128)} %constant.61.clone.1), dimensions={1,2}, to_apply=%all_to_all.12.reduce_sub_computation | reduce | bytes 1028 | tf_op jit(solution)/shard_map/all_to_all | solution.py:33
  36.0 1.0 broadcast_select_fusion
  37.1 9.3 %all-to-all-start.1 = ((s32[128,4,128]{2,1,0:T(4,128)}), s32[128,4,128]{2,1,0:T(4,128)S(1)}, u32[]{:S(2)}, u32[]{:S(2)}) async-start(s32[128,4,128]{2,1,0:T(4,128)} %broadcast_select_fusion), calls=%async_computation.1 | async-start | bytes 524288 | tf_op jit(solution)/shard_map/all_to_all | solution.py:33
  46.4 0.5 slice.8
  48.3 10.2 %all-to-all-done.1 = s32[128,4,128]{2,1,0:T(4,128)S(1)} async-done(((s32[128,4,128]{2,1,0:T(4,128)}), s32[128,4,128]{2,1,0:T(4,128)S(1)}, u32[]{:S(2)}, u32[]{:S(2)}) %all-to-all-start.1) | async-done | bytes 262176 | tf_op jit(solution)/shard_map/all_to_all | solution.py:33
  58.6 0.8 select_reduce_fusion.4
  59.9 0.6 fusion.9
  60.6 63.8 %all-gather.2.cloned.1.call-done.q_hbm = bf16[512,128,256]{2,1,0:T(8,128)(2,1)} async-done(((bf16[4,128,256]{2,1,0:T(8,128)(2,1)}), bf16[512,128,256]{2,1,0:T(8,128)(2,1)}) %all-gather.2.cloned.1.call-update) | async-done | bytes 33554448 | tf_op jit(solution)/shard_map/all_gather | solution.py:226
  124.3 6.0 %totals.1 = (f32[1024,128]{1,0:T(8,128)S(1)}, f32[256,128,128]{2,1,0:T(8,128)S(1)}, bf16[256,128,256]{2,1,0:T(8,128)(2,1)S(1)}) custom-call(s32[256]{0:T(256)S(1)} %get-tuple-element.16.pair_tile, s32[256]{0:T(256)S(1)} %get-tuple-element.20.pair_query, s32[256]{0:T(256)S(1)} %get-tuple-element.19.pair_out, s32[1]{0:T(128)} %bitcast.4.pairs, s32[64]{0:T(128)S(1)} %copy-done, ...), custom_call_target="tpu_custom_call" | custom-call | tf_op jit(solution)/shard_map/totals/pallas_call | solution.py:184
  130.3 22.2 %all_to_all.20.arrived_ref = f32[128,8,128]{2,1,0:T(8,128)S(1)} all-to-all(f32[128,8,128]{2,1,0:T(8,128)S(1)} %bitcast.14), channel_id=1, replica_groups=mesh['cam'=32,'lidar'=4] {'cam','lidar'}, dimensions={0} | all-to-all | bytes 1048576 | tf_op jit(solution)/shard_map/all_to_all | solution.py:33
  152.6 0.8 share.1
  153.3 15.2 %all_to_all.21 = f32[128,4,128]{2,1,0:T(4,128)S(1)} all-to-all(f32[128,4,128]{2,1,0:T(4,128)S(1)} %get-tuple-element.11), channel_id=1, replica_groups=mesh['cam'=32,'lidar'=4] {'cam','lidar'}, dimensions={0} | all-to-all | bytes 524288 | tf_op jit(solution)/shard_map/all_to_all | solution.py:33
  168.6 4.7 %grads.1 = bf16[64,128,256]{2,1,0:T(8,128)(2,1)} custom-call(s32[256]{0:T(256)S(1)} %get-tuple-element.16.pair_tile, s32[256]{0:T(256)S(1)} %get-tuple-element.20.pair_query, s32[1]{0:T(128)} %bitcast.4.pairs, f32[256,128,128]{2,1,0:T(8,128)S(1)} %get-tuple-element.9.expo_ref, bf16[256,128,256]{2,1,0:T(8,128)(2,1)S(1)} %get-tuple-element.10.q_ref, ...), custom_call_target="tpu_custom_call" | custom-call | tf_op jit(solution)/shard_map/grads/pallas_call | solution.py:184
  (24 shorter events, 1.1 us)
Async XLA Ops:
  7.2 41.0 %copy-start.2 = (s32[64]{0:T(128)S(1)}, s32[64]{0:T(128)}, u32[]{:S(2)}) copy-start(s32[64]{0:T(128)} %param.9) | copy-start | bytes 772
  7.2 28.8 %copy-start.1 = (s32[4,128]{1,0:T(4,128)S(1)}, s32[4,128]{1,0:T(4,128)}, u32[]{:S(2)}) copy-start(s32[4,128]{1,0:T(4,128)} %param.13) | copy-start | bytes 6148
  7.2 117.2 %copy-start = (s32[64]{0:T(128)S(1)}, s32[64]{0:T(128)}, u32[]{:S(2)}) copy-start(s32[64]{0:T(128)} %count.1) | copy-start | bytes 772
  7.2 117.2 %all-gather.2.cloned.1.call-start = ((), (), s32[]{:S(2)}) async-start(), calls=%async_computation.4 | async-start | bytes 33816576 | tf_op jit(solution)/shard_map/all_gather | solution.py:226
  12.3 21.1 %all-to-all-start = ((s32[128,1,1]{2,1,0:T(1,128)}), s32[128,1,1]{2,1,0:T(1,128)S(1)}, u32[]{:S(2)}, u32[]{:S(2)}) async-start(s32[128,1,1]{2,1,0:T(1,128)} %copy.28), calls=%async_computation | async-start | bytes 131072 | tf_op jit(solution)/shard_map/all_to_all | solution.py:33
  37.1 21.4 %all-to-all-start.1 = ((s32[128,4,128]{2,1,0:T(4,128)}), s32[128,4,128]{2,1,0:T(4,128)S(1)}, u32[]{:S(2)}, u32[]{:S(2)}) async-start(s32[128,4,128]{2,1,0:T(4,128)} %broadcast_select_fusion), calls=%async_computation.1 | async-start | bytes 524288 | tf_op jit(solution)/shard_map/all_to_all | solution.py:33
Sparse Core Ops, SparseCore 0:
  11.2 113.1 all-gather.1
